TPU v7x, 32 devices: a whole 2x2x4 slice. The times are simulated.
32 devices in a mesh: videos: 4 (over z), mp: 8 (over y, x, core).
Axes of the slice: x: 2, y: 2, z: 4, core: 2. Of those that a mesh axis runs over, the one named last changes fastest.
Arguments:
- frames: bfloat16 [192, 197, 768], P(('videos', 'mp')), may hold values from -8 to 8
- cotangent: bfloat16 [192, 197, 768], P(('videos', 'mp')), may hold values from -6 to 6
- frame_video: int32 [192], P('videos'), may hold values from 0 to 11, as said below
- group_ids: int32 [12], replicated, may hold values from 0 to 5, as said below
- message_fc: bfloat16 [768, 768], P('mp'), may hold values from -0.21875 to 0.21875
- message_gain: bfloat16 [768], P('mp'), may hold values from 0.5 to 1.5
- message_shift: bfloat16 [768], P('mp'), may hold values from -1 to 1
- message_qkv: bfloat16 [768, 2304], P('mp'), may hold values from -0.3125 to 0.3125
- message_out: bfloat16 [768, 768], P('mp'), may hold values from -0.4375 to 0.4375
- pre_gain: bfloat16 [768], P('mp'), may hold values from 0.5 to 1.5
- pre_shift: bfloat16 [768], P('mp'), may hold values from -1 to 1
- attn_qkv: bfloat16 [768, 2304], P('mp'), may hold values from -0.3125 to 0.3125
- attn_out: bfloat16 [768, 768], P('mp'), may hold values from -0.625 to 0.625
- mlp_gain: bfloat16 [768], P('mp'), may hold values from 0.5 to 1.5
- mlp_shift: bfloat16 [768], P('mp'), may hold values from -1 to 1
- fc_in: bfloat16 [768, 3072], P('mp'), may hold values from -0.21875 to 0.21875
- fc_out: bfloat16 [3072, 768], P('mp'), may hold values from -0.109375 to 0.109375
Outputs:
- out_frames: bfloat16 [192, 197, 768], P(('videos', 'mp'))
- clip_loss: float32 [], replicated
- frames_grad: bfloat16 [192, 197, 768], P(('videos', 'mp'))
- grad_message_fc: bfloat16 [768, 768], P('mp')
- grad_message_gain: bfloat16 [768], P('mp')
- grad_message_shift: bfloat16 [768], P('mp')
- grad_message_qkv: bfloat16 [768, 2304], P('mp')
- grad_message_out: bfloat16 [768, 768], P('mp')
- grad_pre_gain: bfloat16 [768], P('mp')
- grad_pre_shift: bfloat16 [768], P('mp')
- grad_attn_qkv: bfloat16 [768, 2304], P('mp')
- grad_attn_out: bfloat16 [768, 768], P('mp')
- grad_mlp_gain: bfloat16 [768], P('mp')
- grad_mlp_shift: bfloat16 [768], P('mp')
- grad_fc_in: bfloat16 [768, 3072], P('mp')
- grad_fc_out: bfloat16 [3072, 768], P('mp')
Inputs may be any that keep to these rules, and one draw needn't show every extreme that they name: `frame_video`: frames of index block g (frames 48 * g to 48 * (g + 1) - 1) belong to videos 3 * g to 3 * (g + 1) - 1, each video having exactly 16 frames. `group_ids`: each value names exactly two videos.
All inputs are finite; a program needn't handle non-finite values.
Results may differ from a plain program's by a relative error of at most 0.029.
Values may be sent and summed in bfloat16 or wider, within the bound.
No kernel may reach another device: no remote copies, remote signals or barrier semaphores. Data moves between devices by JAX's collectives and lax.ppermute only.
A program may use at most 192 MiB of HBM per device.

v0:
```python
import jax
import jax.numpy as jnp
from jax import lax
from jax.sharding import PartitionSpec as P

HEADS = 12
FPV = 16


EPS = 1e-05
LOGIT_SCALE = 50.0


def layer_norm(values_in, gain_in, shift_in):
    row_mean = jnp.mean(values_in, axis=-1, keepdims=True)
    centred = values_in - row_mean
    row_var = jnp.mean(centred * centred, axis=-1, keepdims=True)
    return centred * lax.rsqrt(row_var + EPS) * gain_in + shift_in


def quick_gelu(values_in):
    return values_in * jax.nn.sigmoid(1.702 * values_in)


def contrast(pooled, group_ids):
    centred = pooled - jnp.mean(pooled, axis=0, keepdims=True)
    embed = centred * lax.rsqrt(jnp.sum(centred * centred, axis=1, keepdims=True) + 1e-06)
    logits = LOGIT_SCALE * jnp.dot(embed, embed.T, precision=lax.Precision.HIGHEST)
    count_videos = pooled.shape[0]
    diagonal = jnp.arange(count_videos)[:, None] == jnp.arange(count_videos)[None, :]
    others = jnp.where(diagonal, -1e30, logits)
    log_total = jax.nn.logsumexp(others, axis=1)
    positive = jnp.logical_and(group_ids[:, None] == group_ids[None, :], jnp.logical_not(diagonal))
    pos_count = jnp.sum(positive.astype(jnp.float32), axis=1)
    pos_mean = jnp.sum(jnp.where(positive, logits, 0.0), axis=1) / pos_count
    return jnp.mean(log_total - pos_mean)


def softmax_back(probs_full, prob_grad):
    row_dot = jnp.sum(prob_grad * probs_full, axis=-1, keepdims=True)
    return (probs_full * (prob_grad - row_dot)).astype(jnp.bfloat16)


def local(
    frames,
    cotangent,
    frame_video,
    group_ids,
    message_fc,
    message_gain,
    message_shift,
    message_qkv,
    message_out,
    pre_gain,
    pre_shift,
    attn_qkv,
    attn_out,
    mlp_gain,
    mlp_shift,
    fc_in,
    fc_out,
):
    f32 = jnp.float32
    bf16 = jnp.bfloat16
    count_frames, patches, features = frames.shape
    head_dim = features // HEADS
    score_scale = head_dim ** (-0.5)
    group_frames = frame_video.shape[0]
    group_videos = group_frames // FPV
    gathered = (
        lax.all_gather(message_fc, "mp", axis=0, tiled=True),
        lax.all_gather(message_gain, "mp", axis=0, tiled=True),
        lax.all_gather(message_shift, "mp", axis=0, tiled=True),
        lax.all_gather(message_qkv, "mp", axis=0, tiled=True),
        lax.all_gather(message_out, "mp", axis=0, tiled=True),
        lax.all_gather(pre_gain, "mp", axis=0, tiled=True),
        lax.all_gather(pre_shift, "mp", axis=0, tiled=True),
        lax.all_gather(attn_qkv, "mp", axis=0, tiled=True),
        lax.all_gather(attn_out, "mp", axis=0, tiled=True),
        lax.all_gather(mlp_gain, "mp", axis=0, tiled=True),
        lax.all_gather(mlp_shift, "mp", axis=0, tiled=True),
        lax.all_gather(fc_in, "mp", axis=0, tiled=True),
        lax.all_gather(fc_out, "mp", axis=0, tiled=True),
    )
    (
        fc_msg_w,
        msg_gain_w,
        msg_shift_w,
        mqkv_w,
        mout_w,
        pre_gain_w,
        pre_shift_w,
        qkv_w,
        out_w,
        mlp_gain_w,
        mlp_shift_w,
        fc_in_w,
        fc_out_w,
    ) = gathered
    msg_gain_f = msg_gain_w.astype(f32)
    msg_shift_f = msg_shift_w.astype(f32)
    pre_gain_f = pre_gain_w.astype(f32)
    pre_shift_f = pre_shift_w.astype(f32)
    mlp_gain_f = mlp_gain_w.astype(f32)
    mlp_shift_f = mlp_shift_w.astype(f32)
    own_video = lax.dynamic_slice_in_dim(
        frame_video, lax.axis_index("mp") * count_frames, count_frames
    )
    video_base = lax.axis_index("videos") * group_videos
    own_onehot = (own_video[:, None] - video_base == jnp.arange(group_videos)[None, :]).astype(f32)
    same_video = own_video[:, None] == frame_video[None, :]
    class_tok = frames[:, 0, :]
    message = jnp.dot(class_tok, fc_msg_w, preferred_element_type=f32)
    msg_act = layer_norm(message, msg_gain_f, msg_shift_f).astype(bf16)
    msg_proj = jnp.dot(msg_act, mqkv_w, preferred_element_type=f32).astype(bf16)
    msg_query = msg_proj[:, :features].reshape(count_frames, HEADS, head_dim)
    kv_group = lax.all_gather(msg_proj[:, features:], "mp", axis=0, tiled=True)
    key_group = kv_group[:, :features].reshape(group_frames, HEADS, head_dim)
    value_group = kv_group[:, features:].reshape(group_frames, HEADS, head_dim)
    msg_scores = (
        jnp.einsum("fhd,ghd->hfg", msg_query, key_group, preferred_element_type=f32) * score_scale
    )
    msg_probs = jax.nn.softmax(jnp.where(same_video[None], msg_scores, -1e30), axis=-1)
    msg_probs_low = msg_probs.astype(bf16)
    msg_mix = (
        jnp.einsum("hfg,ghd->fhd", msg_probs_low, value_group, preferred_element_type=f32)
        .reshape(count_frames, features)
        .astype(bf16)
    )
    msg_total = message + jnp.dot(msg_mix, mout_w, preferred_element_type=f32)
    stacked = jnp.concatenate([frames.astype(f32), msg_total[:, None, :]], axis=1)
    pre_act = layer_norm(stacked, pre_gain_f, pre_shift_f).astype(bf16)
    qkv_all = (
        jnp.dot(pre_act.reshape(-1, features), qkv_w, preferred_element_type=f32)
        .astype(bf16)
        .reshape(count_frames, patches + 1, 3 * features)
    )
    frame_query = qkv_all[:, :patches, :features].reshape(count_frames, patches, HEADS, head_dim)
    frame_key = qkv_all[:, :, features : 2 * features].reshape(
        count_frames, patches + 1, HEADS, head_dim
    )
    frame_value = qkv_all[:, :, 2 * features :].reshape(count_frames, patches + 1, HEADS, head_dim)
    frame_scores = (
        jnp.einsum("fqhd,fkhd->fhqk", frame_query, frame_key, preferred_element_type=f32)
        * score_scale
    )
    log_total = jax.nn.logsumexp(frame_scores, axis=-1, keepdims=True)
    frame_probs = jnp.exp(frame_scores - log_total).astype(bf16)
    frame_mixed = (
        jnp.einsum("fhqk,fkhd->fqhd", frame_probs, frame_value, preferred_element_type=f32)
        .reshape(count_frames * patches, features)
        .astype(bf16)
    )
    residual = stacked[:, :patches, :].reshape(count_frames * patches, features) + jnp.dot(
        frame_mixed, out_w, preferred_element_type=f32
    )
    mlp_act = layer_norm(residual, mlp_gain_f, mlp_shift_f).astype(bf16)
    hidden_pre = jnp.dot(mlp_act, fc_in_w, preferred_element_type=f32)
    hidden = quick_gelu(hidden_pre).astype(bf16)
    output = residual + jnp.dot(hidden, fc_out_w, preferred_element_type=f32)
    out_frames = output.reshape(count_frames, patches, features).astype(bf16)
    frame_mean = jnp.mean(output.reshape(count_frames, patches, features), axis=1)
    video_part = jnp.dot(own_onehot.T, frame_mean, precision=lax.Precision.HIGHEST) / FPV
    video_sums = lax.psum(video_part, "mp")
    all_pooled = lax.all_gather(video_sums, "videos", axis=0, tiled=True)
    count_videos = all_pooled.shape[0]
    clip_loss, loss_back = jax.vjp(lambda pooled: contrast(pooled, group_ids), all_pooled)
    pooled_grad = loss_back(jnp.full_like(clip_loss, float(count_videos * FPV * patches)))[0]
    own_grad = lax.dynamic_slice_in_dim(pooled_grad, video_base, group_videos, 0)
    frame_grad = jnp.dot(own_onehot, own_grad, precision=lax.Precision.HIGHEST) / (FPV * patches)
    output_grad = (cotangent.astype(f32) + frame_grad[:, None, :]).reshape(
        count_frames * patches, features
    )
    back_set = (
        lax.all_gather(message_fc, "mp", axis=0, tiled=True),
        lax.all_gather(message_gain, "mp", axis=0, tiled=True),
        lax.all_gather(message_shift, "mp", axis=0, tiled=True),
        lax.all_gather(message_qkv, "mp", axis=0, tiled=True),
        lax.all_gather(message_out, "mp", axis=0, tiled=True),
        lax.all_gather(pre_gain, "mp", axis=0, tiled=True),
        lax.all_gather(pre_shift, "mp", axis=0, tiled=True),
        lax.all_gather(attn_qkv, "mp", axis=0, tiled=True),
        lax.all_gather(attn_out, "mp", axis=0, tiled=True),
        lax.all_gather(mlp_gain, "mp", axis=0, tiled=True),
        lax.all_gather(mlp_shift, "mp", axis=0, tiled=True),
        lax.all_gather(fc_in, "mp", axis=0, tiled=True),
        lax.all_gather(fc_out, "mp", axis=0, tiled=True),
    )
    fc_msg_b = back_set[0]
    mqkv_b = back_set[3]
    mout_b = back_set[4]
    qkv_b = back_set[7]
    out_b = back_set[8]
    fc_in_b = back_set[11]
    fc_out_b = back_set[12]
    branch_grad = output_grad.astype(bf16)
    grad_fc_out = jnp.einsum("rf,rd->fd", hidden, branch_grad, preferred_element_type=f32)
    hidden_grad = jnp.einsum("rd,fd->rf", branch_grad, fc_out_b, preferred_element_type=f32)
    gelu_back = jax.vjp(quick_gelu, hidden_pre)[1]
    hidden_pre_grad = gelu_back(hidden_grad)[0].astype(bf16)
    grad_fc_in = jnp.einsum("rd,rf->df", mlp_act, hidden_pre_grad, preferred_element_type=f32)
    normed_grad = jnp.einsum("rf,df->rd", hidden_pre_grad, fc_in_b, preferred_element_type=f32)
    mlp_back = jax.vjp(layer_norm, residual, mlp_gain_f, mlp_shift_f)[1]
    residual_part, grad_mlp_gain, grad_mlp_shift = mlp_back(normed_grad)
    residual_grad = output_grad + residual_part
    attn_grad = residual_grad.astype(bf16)
    grad_attn_out = jnp.einsum("rc,rd->cd", frame_mixed, attn_grad, preferred_element_type=f32)
    mixed_grad = (
        jnp.einsum("rd,cd->rc", attn_grad, out_b, preferred_element_type=f32)
        .astype(bf16)
        .reshape(count_frames, patches, HEADS, head_dim)
    )
    again_scores = (
        jnp.einsum("fqhd,fkhd->fhqk", frame_query, frame_key, preferred_element_type=f32)
        * score_scale
    )
    probs_full = jnp.exp(again_scores - log_total)
    prob_grad = jnp.einsum("fqhd,fkhd->fhqk", mixed_grad, frame_value, preferred_element_type=f32)
    value_grad = jnp.einsum(
        "fhqk,fqhd->fkhd", probs_full.astype(bf16), mixed_grad, preferred_element_type=f32
    )
    score_grad = softmax_back(probs_full, prob_grad)
    query_grad = (
        jnp.einsum("fhqk,fkhd->fqhd", score_grad, frame_key, preferred_element_type=f32)
        * score_scale
    )
    key_grad = (
        jnp.einsum("fhqk,fqhd->fkhd", score_grad, frame_query, preferred_element_type=f32)
        * score_scale
    )
    query_rows = jnp.pad(
        query_grad.reshape(count_frames, patches, features), ((0, 0), (0, 1), (0, 0))
    )
    qkv_grad = (
        jnp.concatenate(
            [
                query_rows,
                key_grad.reshape(count_frames, patches + 1, features),
                value_grad.reshape(count_frames, patches + 1, features),
            ],
            axis=2,
        )
        .astype(bf16)
        .reshape(-1, 3 * features)
    )
    grad_attn_qkv = jnp.einsum(
        "rd,rc->dc", pre_act.reshape(-1, features), qkv_grad, preferred_element_type=f32
    )
    pre_grad = jnp.einsum("rc,dc->rd", qkv_grad, qkv_b, preferred_element_type=f32).reshape(
        count_frames, patches + 1, features
    )
    pre_back = jax.vjp(layer_norm, stacked, pre_gain_f, pre_shift_f)[1]
    stacked_part, grad_pre_gain, grad_pre_shift = pre_back(pre_grad)
    patch_grad = stacked_part[:, :patches, :] + residual_grad.reshape(
        count_frames, patches, features
    )
    total_grad_full = stacked_part[:, patches, :]
    total_grad = total_grad_full.astype(bf16)
    grad_message_out = jnp.einsum("fc,fd->cd", msg_mix, total_grad, preferred_element_type=f32)
    msg_mix_grad = (
        jnp.einsum("fd,cd->fc", total_grad, mout_b, preferred_element_type=f32)
        .astype(bf16)
        .reshape(count_frames, HEADS, head_dim)
    )
    msg_prob_grad = jnp.einsum(
        "fhd,ghd->hfg", msg_mix_grad, value_group, preferred_element_type=f32
    )
    msg_value_grad = jnp.einsum(
        "hfg,fhd->ghd", msg_probs_low, msg_mix_grad, preferred_element_type=f32
    )
    msg_score_grad = softmax_back(msg_probs, msg_prob_grad)
    msg_query_grad = (
        jnp.einsum("hfg,ghd->fhd", msg_score_grad, key_group, preferred_element_type=f32)
        * score_scale
    )
    msg_key_grad = (
        jnp.einsum("hfg,fhd->ghd", msg_score_grad, msg_query, preferred_element_type=f32)
        * score_scale
    )
    kv_terms = jnp.concatenate(
        [
            msg_key_grad.reshape(group_frames, features),
            msg_value_grad.reshape(group_frames, features),
        ],
        axis=1,
    )
    kv_grad = lax.psum_scatter(kv_terms, "mp", scatter_dimension=0, tiled=True)
    msg_qkv_grad = jnp.concatenate(
        [msg_query_grad.reshape(count_frames, features), kv_grad], axis=1
    ).astype(bf16)
    grad_message_qkv = jnp.einsum("fd,fc->dc", msg_act, msg_qkv_grad, preferred_element_type=f32)
    msg_norm_grad = jnp.einsum("fc,dc->fd", msg_qkv_grad, mqkv_b, preferred_element_type=f32)
    msg_back = jax.vjp(layer_norm, message, msg_gain_f, msg_shift_f)[1]
    message_part, grad_message_gain, grad_message_shift = msg_back(msg_norm_grad)
    message_grad = (total_grad_full + message_part).astype(bf16)
    grad_message_fc = jnp.einsum("fd,fc->dc", class_tok, message_grad, preferred_element_type=f32)
    class_grad = jnp.einsum("fc,dc->fd", message_grad, fc_msg_b, preferred_element_type=f32)
    frames_grad = patch_grad.at[:, 0, :].add(class_grad).astype(bf16)
    weight_grads = (
        grad_message_fc,
        grad_message_gain,
        grad_message_shift,
        grad_message_qkv,
        grad_message_out,
        grad_pre_gain,
        grad_pre_shift,
        grad_attn_qkv,
        grad_attn_out,
        grad_mlp_gain,
        grad_mlp_shift,
        grad_fc_in,
        grad_fc_out,
    )
    shares = (
        lax.psum_scatter(weight_grads[0], "mp", scatter_dimension=0, tiled=True),
        lax.psum_scatter(weight_grads[1], "mp", scatter_dimension=0, tiled=True),
        lax.psum_scatter(weight_grads[2], "mp", scatter_dimension=0, tiled=True),
        lax.psum_scatter(weight_grads[3], "mp", scatter_dimension=0, tiled=True),
        lax.psum_scatter(weight_grads[4], "mp", scatter_dimension=0, tiled=True),
        lax.psum_scatter(weight_grads[5], "mp", scatter_dimension=0, tiled=True),
        lax.psum_scatter(weight_grads[6], "mp", scatter_dimension=0, tiled=True),
        lax.psum_scatter(weight_grads[7], "mp", scatter_dimension=0, tiled=True),
        lax.psum_scatter(weight_grads[8], "mp", scatter_dimension=0, tiled=True),
        lax.psum_scatter(weight_grads[9], "mp", scatter_dimension=0, tiled=True),
        lax.psum_scatter(weight_grads[10], "mp", scatter_dimension=0, tiled=True),
        lax.psum_scatter(weight_grads[11], "mp", scatter_dimension=0, tiled=True),
        lax.psum_scatter(weight_grads[12], "mp", scatter_dimension=0, tiled=True),
    )
    finals = lax.psum(
        (
            shares[0],
            shares[1],
            shares[2],
            shares[3],
            shares[4],
            shares[5],
            shares[6],
            shares[7],
            shares[8],
            shares[9],
            shares[10],
            shares[11],
            shares[12],
        ),
        "videos",
    )
    low_finals = tuple((final_piece.astype(bf16) for final_piece in finals))
    return (
        out_frames,
        clip_loss,
        frames_grad,
        low_finals[0],
        low_finals[1],
        low_finals[2],
        low_finals[3],
        low_finals[4],
        low_finals[5],
        low_finals[6],
        low_finals[7],
        low_finals[8],
        low_finals[9],
        low_finals[10],
        low_finals[11],
        low_finals[12],
    )


def solution(mesh):
    return jax.shard_map(
        local,
        mesh=mesh,
        in_specs=(
            P(("videos", "mp"), None, None),
            P(("videos", "mp"), None, None),
            P("videos"),
            P(),
            P("mp", None),
            P("mp"),
            P("mp"),
            P("mp", None),
            P("mp", None),
            P("mp"),
            P("mp"),
            P("mp", None),
            P("mp", None),
            P("mp"),
            P("mp"),
            P("mp", None),
            P("mp", None),
        ),
        out_specs=(
            P(("videos", "mp"), None, None),
            P(),
            P(("videos", "mp"), None, None),
            P("mp", None),
            P("mp"),
            P("mp"),
            P("mp", None),
            P("mp", None),
            P("mp"),
            P("mp"),
            P("mp", None),
            P("mp", None),
            P("mp"),
            P("mp"),
            P("mp", None),
            P("mp", None),
        ),
        check_vma=False,
    )
```

profile of v0, /device:TPU:0, one launch (start us, length us, event | category | flops | bytes accessed | tf_op | source)
XLA Modules:
  0.0 1018.1 jit_solution(7992255852160035602)
XLA Ops:
  20.0 25.7 %all-reduce.17 = (bf16[768]{0:T(1024)(128)(2,1)S(1)}, bf16[768]{0:T(1024)(128)(2,1)S(1)}, bf16[768]{0:T(1024)(128)(2,1)S(1)}, bf16[768]{0:T(1024)(128)(2,1)S(1)}...) all-reduce(bf16[768]{0:T(1024)(128)(2,1)S(1)} %dynamic-update-slice, ...), channel_id=1, replica_groups=mesh['videos'=4,'mp'=8] {'mp'}, use_global_device_ids=true, to_apply=%add.2 | all-reduce | flops 4608 | bytes 18432
  47.9 24.8 %all-gather.12.cloned.1.call-done = bf16[768,2304]{1,0:T(8,128)(2,1)} async-done(((bf16[96,2304]{1,0:T(8,128)(2,1)}), bf16[768,2304]{1,0:T(8,128)(2,1)}) %all-gather.12.cloned.1.call-update) | async-done | bytes 3538960 | tf_op jit(solution)/shard_map/all_gather | solution.py:74
  75.4 9.2 all-gather
  86.6 12.1 %all-gather.14.cloned.1.call-done = bf16[768,768]{1,0:T(8,128)(2,1)} async-done(((bf16[96,768]{1,0:T(8,128)(2,1)}), bf16[768,768]{1,0:T(8,128)(2,1)}) %all-gather.14.cloned.1.call-update) | async-done | bytes 1179664 | tf_op jit(solution)/shard_map/all_gather | solution.py:75
  111.6 22.8 %all-gather.16.cloned.1.call-done = bf16[768,2304]{1,0:T(8,128)(2,1)} async-done(((bf16[96,2304]{1,0:T(8,128)(2,1)}), bf16[768,2304]{1,0:T(8,128)(2,1)}) %all-gather.16.cloned.1.call-update) | async-done | bytes 3538960 | tf_op jit(solution)/shard_map/all_gather | solution.py:78
  134.4 10.2 %convolution_convert_fusion = bf16[1188,2304]{1,0:T(8,128)(2,1)} fusion(bf16[768,2304]{1,0:T(8,128)(2,1)} %all-gather.16.cloned.1.call-done, f32[1188,768]{1,0:T(8,128)} %concatenate.25, f32[768]{0:T(1024)S(1)} %convert_element_type.169, f32[768]{0:T(1024)S(1)} %convert_element_type.168, f32[1188]{0:T(1024)S(1)} %rsqrt.49, f32[1188]{0:T(1024)S(1)} %div.121), kind=kOutput, calls=%fused_computation.13 | convolution fusion | flops 4211564544 | bytes 12678432 | tf_op jit(solution)/shard_map/dot_general | solution.py:134
  144.6 5.4 reshape.336
  165.9 5.5 multiply_reduce_fusion.1
  200.9 14.5 %multiply_convert_fusion.1 = (bf16[1182,3072]{1,0:T(8,128)(2,1)}, f32[1182,3072]{1,0:T(8,128)}) fusion(bf16[768,3072]{1,0:T(8,128)(2,1)} %all-gather.20.cloned.1.call-done, f32[1182,768]{1,0:T(8,128)} %copy-done.8, f32[768]{0:T(1024)S(1)} %convert_element_type.177, f32[768]{0:T(1024)S(1)} %convert_element_type.176, f32[1182]{0:T(1024)S(1)} %fusion.75, ...), kind=kOutput, calls=%fused_computation.10 | convolution fusion | flops 5603701248 | bytes 30151920 | tf_op jit(solution)/shard_map/dot_general | solution.py:158
  215.4 26.3 %all-gather.22.cloned.1.call-done = bf16[3072,768]{1,0:T(8,128)(2,1)} async-done(((bf16[384,768]{1,0:T(8,128)(2,1)}), bf16[3072,768]{1,0:T(8,128)(2,1)}) %all-gather.22.cloned.1.call-update) | async-done | bytes 4718608 | tf_op jit(solution)/shard_map/all_gather | solution.py:83
  241.8 11.6 %convolution_add_fusion = f32[1182,768]{1,0:T(8,128)} fusion(f32[1182,768]{1,0:T(8,128)} %copy-done.8, bf16[1182,3072]{1,0:T(8,128)(2,1)} %get-tuple-element.176, bf16[3072,768]{1,0:T(8,128)(2,1)} %all-gather.22.cloned.1.call-done), kind=kOutput, calls=%fused_computation.24 | convolution fusion | flops 5578283520 | bytes 19243008 | tf_op jit(solution)/shard_map/dot_general | solution.py:160
  262.7 23.5 %psum.98 = f32[3,768]{1,0:T(4,128)S(1)} all-reduce(f32[3,768]{1,0:T(4,128)S(1)} %convolution_multiply_fusion.4), channel_id=1, replica_groups=mesh['videos'=4,'mp'=8] {'mp'}, use_global_device_ids=true, to_apply=%region_11.12 | all-reduce | flops 2304 | bytes 18432 | tf_op jit(solution)/shard_map/psum | solution.py:164
  286.2 13.1 %all-gather.1 = f32[4,3,768]{2,1,0:T(4,128)S(1)} all-gather(f32[1,3,768]{2,1,0:T(4,128)S(1)} %bitcast.103), channel_id=1, replica_groups=mesh['videos'=4,'mp'=8] {'videos'}, dimensions={0}, use_global_device_ids=true | all-gather | bytes 46080 | tf_op jit(solution)/shard_map/all_gather | solution.py:165
  308.0 16.4 %fusion.5 = bf16[1182,3072]{1,0:T(8,128)(2,1)} fusion(f32[1182,3072]{1,0:T(8,128)} %get-tuple-element.177, bf16[3072,768]{1,0:T(8,128)(2,1)} %all-gather.22.cloned.1.call-done, f32[1182,768]{1,0:T(8,128)} %reshape.341), kind=kOutput, calls=%fused_computation.9 | convolution fusion | flops 5621856768 | bytes 30136320 | tf_op jit(solution)/shard_map/rd,fd->rf/dot_general | solution.py:198
  324.4 10.4 %multiply_reduce_fusion.5 = (f32[768]{0:T(1024)}, f32[1182]{0:T(1024)S(1)}, f32[768]{0:T(1024)}, f32[1182,768]{1,0:T(8,128)S(1)}) fusion(f32[1182,768]{1,0:T(8,128)S(1)} %copy-done.9, f32[1182]{0:T(1024)S(1)} %fusion.75, f32[1182]{0:T(1024)S(1)} %broadcast_multiply_fusion, f32[768]{0:T(1024)S(1)} %convert_element_type.176, bf16[1182,3072]{1,0:T(8,128)(2,1)} %fusion.5, ...), kind=kOutput, calls=%fused_computation.34 | convolution fusion | flops 5584634880 | bytes 19266408 | tf_op jit(solution)/shard_map/rf,df->rd/dot_general | solution.py:202
  345.8 5.6 copy.167
  351.4 13.0 %multiply_reduce_fusion = (f32[6,12,197]{2,1,0:T(8,128)S(1)}, f32[6,12,197,198]{3,2,1,0:T(8,128)}) fusion(f32[6,12,197,198]{3,2,1,0:T(8,128)} %copy-done, f32[6,12,197]{2,1,0:T(8,128)S(1)} %log_add_fusion, bf16[6,197,12,64]{1,3,2,0:T(8,128)(2,1)S(1)} %copy.167, bf16[6,198,12,64]{1,3,2,0:T(8,128)(2,1)} %bitcast.96), kind=kOutput, calls=%fused_computation.3 | convolution fusion | flops 370698880 | bytes 26221248 | tf_op jit(solution)/shard_map/fqhd,fkhd->fhqk/dot_general | solution.py:218
  364.4 7.9 convolution_convert_fusion.3
  375.5 11.7 %multiply_convert_fusion = bf16[6,12,197,198]{3,2,1,0:T(8,128)(2,1)S(1)} fusion(f32[6,12,197,198]{3,2,1,0:T(8,128)} %get-tuple-element.184, f32[6,12,197,198]{3,2,1,0:T(8,128)} %copy-done, f32[6,12,197]{2,1,0:T(8,128)S(1)} %get-tuple-element.183, f32[6,12,197]{2,1,0:T(8,128)S(1)} %log_add_fusion), kind=kLoop, calls=%fused_computation.2 | loop fusion | flops 14042160 | bytes 28197792 | tf_op jit(solution)/shard_map/convert_element_type | solution.py:41
  396.8 6.9 multiply_convert_fusion.3
  408.1 9.3 fusion.98
  444.7 15.5 %fusion = f32[8,1536]{1,0:T(8,128)} fusion(f32[48,1536]{1,0:T(8,128)} %pad_maximum_fusion.1), kind=kCustom, calls=%all-reduce-scatter | all-reduce-scatter fusion | flops 98305 | bytes 344576
  481.6 11.8 %convolution_bitcast_fusion = f32[768,2304]{1,0:T(8,128)} fusion(f32[6,198,768]{2,1,0:T(8,128)} %get-tuple-element.155, f32[768]{0:T(1024)S(1)} %copy-done.71, f32[6,198]{1,0:T(8,128)S(1)} %copy-done.39, f32[768]{0:T(1024)S(1)} %copy-done.52, f32[6,198]{1,0:T(8,128)S(1)} %copy-done.33, bf16[6,197,768]{2,1,0:T(8,128)(2,1)} %copy.168, ...), kind=kOutput, calls=%fused_computation.17 | convolution fusion | flops 4230724608 | bytes 16208160 | tf_op jit(solution)/shard_map/rd,rc->dc/dot_general | solution.py:246
  499.0 12.9 %fusion.96 = f32[768,3072]{1,0:T(8,128)} fusion(bf16[1182,3072]{1,0:T(8,128)(2,1)} %fusion.5, f32[1182,768]{1,0:T(8,128)} %copy-done.8, f32[768]{0:T(1024)S(1)} %copy-done.69, f32[768]{0:T(1024)S(1)} %copy-done.59, f32[1182]{0:T(1024)S(1)} %copy-done.54, f32[1182]{0:T(1024)S(1)} %copy-done.47), kind=kOutput, calls=%fused_computation.190 | convolution fusion | flops 5581914624 | bytes 20346096 | tf_op jit(solution)/shard_map/rd,rf->df/dot_general | solution.py:201
  512.1 11.9 %fusion.34 = f32[3072,768]{1,0:T(8,128)} fusion(bf16[1182,3072]{1,0:T(8,128)(2,1)} %get-tuple-element.176, f32[1182,768]{1,0:T(8,128)} %reshape.341), kind=kOutput, calls=%fused_computation.76 | convolution fusion | flops 5578283520 | bytes 20330496 | tf_op jit(solution)/shard_map/rf,rd->fd/dot_general | solution.py:197
  530.0 5.6 slice_add_fusion
  535.7 24.7 %all-reduce.15 = (f32[768]{0:T(1024)S(1)}, f32[768]{0:T(1024)S(1)}, f32[768]{0:T(1024)S(1)}, f32[768]{0:T(1024)S(1)}, f32[768]{0:T(1024)S(1)}, /*index=5*/f32[768]{0:T(1024)S(1)}) all-reduce(f32[768]{0:T(1024)S(1)} %copy-done.61, f32[768]{0:T(1024)S(1)} %copy-done.62, ...), channel_id=4, replica_groups=mesh['videos'=4,'mp'=8] {'mp'}, use_global_device_ids=true, to_apply=%region_33.34.clone | all-reduce | flops 4608 | bytes 36864
  568.4 33.1 %reduce-scatter.16.cloned.1.call-done = f32[96,2304]{1,0:T(8,128)} async-done(((f32[768,2304]{1,0:T(8,128)}), f32[96,2304]{1,0:T(8,128)}) %reduce-scatter.16.cloned.1.call-update) | async-done | bytes 884752 | tf_op jit(solution)/shard_map/reduce_scatter | solution.py:322
  601.5 68.9 %reduce-scatter.12.cloned.1.call-done = f32[96,2304]{1,0:T(8,128)} async-done(((f32[768,2304]{1,0:T(8,128)}), f32[96,2304]{1,0:T(8,128)}) %reduce-scatter.12.cloned.1.call-update) | async-done | bytes 884752 | tf_op jit(solution)/shard_map/reduce_scatter | solution.py:318
  670.4 80.4 %reduce-scatter.20.cloned.1.call-done = f32[96,3072]{1,0:T(8,128)} async-done(((f32[768,3072]{1,0:T(8,128)}), f32[96,3072]{1,0:T(8,128)}) %reduce-scatter.20.cloned.1.call-update) | async-done | bytes 1179664 | tf_op jit(solution)/shard_map/reduce_scatter | solution.py:326
  750.8 80.3 %reduce-scatter.22.cloned.1.call-done = f32[384,768]{1,0:T(8,128)} async-done(((f32[3072,768]{1,0:T(8,128)}), f32[384,768]{1,0:T(8,128)}) %reduce-scatter.22.cloned.1.call-update) | async-done | bytes 1179664 | tf_op jit(solution)/shard_map/reduce_scatter | solution.py:327
  831.1 178.4 %all-reduce.19 = (bf16[96,768]{0,1:T(8,128)(2,1)S(1)}, bf16[96]{0:T(256)(128)(2,1)}, bf16[96]{0:T(256)(128)(2,1)}, bf16[96,2304]{1,0:T(8,128)(2,1)}, bf16[96,768...) all-reduce(f32[96,768]{0,1:T(8,128)S(1)} %copy.186, ...), channel_id=1, replica_groups=mesh['videos'=4,'mp'=8] {'videos'}, use_global_device_ids=true, to_apply=%region_31.32 | all-reduce | flops 1253952 | bytes 7523712 | tf_op jit(solution)/shard_map/psum | solution.py:329
  (354 shorter events, 189.8 us)
Async XLA Ops:
  7.2 38.8 %all-gather.10.cloned.1.call-start = ((), (), s32[]{:S(2)}) async-start(), calls=%async_computation.7 | async-start | bytes 1327104 | tf_op jit(solution)/shard_map/all_gather | solution.py:71
  7.9 64.8 %all-gather.12.cloned.1.call-start = ((), (), s32[]{:S(2)}) async-start(), calls=%async_computation.8 | async-start | bytes 3981312 | tf_op jit(solution)/shard_map/all_gather | solution.py:74
  8.7 90.0 %all-gather.14.cloned.1.call-start = ((), (), s32[]{:S(2)}) async-start(), calls=%async_computation.9 | async-start | bytes 1327104 | tf_op jit(solution)/shard_map/all_gather | solution.py:75
  9.4 125.0 %all-gather.16.cloned.1.call-start = ((), (), s32[]{:S(2)}) async-start(), calls=%async_computation.10 | async-start | bytes 3981312 | tf_op jit(solution)/shard_map/all_gather | solution.py:78
  10.0 179.0 %all-gather.18.cloned.1.call-start = ((), (), s32[]{:S(2)}) async-start(), calls=%async_computation.11 | async-start | bytes 1327104 | tf_op jit(solution)/shard_map/all_gather | solution.py:79
  10.6 190.4 %all-gather.20.cloned.1.call-start = ((), (), s32[]{:S(2)}) async-start(), calls=%async_computation.12 | async-start | bytes 5308416 | tf_op jit(solution)/shard_map/all_gather | solution.py:82
  11.1 230.6 %all-gather.22.cloned.1.call-start = ((), (), s32[]{:S(2)}) async-start(), calls=%async_computation.13 | async-start | bytes 5308416 | tf_op jit(solution)/shard_map/all_gather | solution.py:83
  11.9 555.4 %reduce-scatter.18.cloned.1.call-start = ((), (), s32[]{:S(2)}) async-start(), calls=%async_computation.17 | async-start | bytes 2654208 | tf_op jit(solution)/shard_map/reduce_scatter | solution.py:323
  12.9 33.1 %copy-start.43 = (bf16[6,1,768]{2,1,0:T(2,128)(2,1)}, bf16[6,1,768]{2,1,0:T(2,128)(2,1)S(1)}, u32[]{:S(2)}) copy-start(bf16[6,1,768]{2,1,0:T(2,128)(2,1)S(1)} %slice.52) | copy-start | bytes 27652
  45.9 88.5 %copy-start.51 = (f32[768]{0:T(1024)}, f32[768]{0:T(1024)S(1)}, u32[]{:S(2)}) copy-start(f32[768]{0:T(1024)S(1)} %convert_element_type.168) | copy-start | bytes 9220
  45.9 88.5 %copy-start.70 = (f32[768]{0:T(1024)}, f32[768]{0:T(1024)S(1)}, u32[]{:S(2)}) copy-start(f32[768]{0:T(1024)S(1)} %convert_element_type.169) | copy-start | bytes 9220
  45.9 289.0 %copy-start.58 = (f32[768]{0:T(1024)}, f32[768]{0:T(1024)S(1)}, u32[]{:S(2)}) copy-start(f32[768]{0:T(1024)S(1)} %convert_element_type.176) | copy-start | bytes 9220
  45.9 155.0 %copy-start.68 = (f32[768]{0:T(1024)}, f32[768]{0:T(1024)S(1)}, u32[]{:S(2)}) copy-start(f32[768]{0:T(1024)S(1)} %convert_element_type.177) | copy-start | bytes 9220
  47.7 56.8 %copy-start.19 = (f32[6,768]{1,0:T(8,128)}, f32[6,768]{1,0:T(8,128)S(1)}, u32[]{:S(2)}) copy-start(f32[6,768]{1,0:T(8,128)S(1)} %get-tuple-element.169) | copy-start | bytes 55300
  47.9 38.0 %copy-start.76 = (f32[6]{0:T(128)}, f32[6]{0:T(128)S(1)}, u32[]{:S(2)}) copy-start(f32[6]{0:T(128)S(1)} %multiply_reduce_fusion.13) | copy-start | bytes 76
  111.4 33.2 %copy-start.48 = (f32[6,198]{1,0:T(8,128)}, f32[6,198]{1,0:T(8,128)S(1)}, u32[]{:S(2)}) copy-start(f32[6,198]{1,0:T(8,128)S(1)} %multiply_reduce_fusion.4) | copy-start | bytes 14260
  111.5 33.1 %copy-start.37 = (f32[6,198]{1,0:T(8,128)}, f32[6,198]{1,0:T(8,128)S(1)}, u32[]{:S(2)}) copy-start(f32[6,198]{1,0:T(8,128)S(1)} %fusion.74) | copy-start | bytes 14260
  194.0 140.9 %copy-start.46 = (f32[1182]{0:T(1024)}, f32[1182]{0:T(1024)S(1)}, u32[]{:S(2)}) copy-start(f32[1182]{0:T(1024)S(1)} %broadcast_multiply_fusion) | copy-start | bytes 14188
  196.3 138.6 %copy-start.53 = (f32[1182]{0:T(1024)}, f32[1182]{0:T(1024)S(1)}, u32[]{:S(2)}) copy-start(f32[1182]{0:T(1024)S(1)} %fusion.75) | copy-start | bytes 14188
  257.6 42.2 %copy-start.66 = (s32[12]{0:T(128)S(1)}, s32[12]{0:T(128)}, u32[]{:S(2)}) copy-start(s32[12]{0:T(128)} %param.22) | copy-start | bytes 148
  257.6 43.9 %copy-start.18 = (bf16[6,197,768]{2,1,0:T(8,128)(2,1)S(1)}, bf16[6,197,768]{2,1,0:T(8,128)(2,1)}, u32[]{:S(2)}) copy-start(bf16[6,197,768]{2,1,0:T(8,128)(2,1)} %param.20) | copy-start | bytes 5446660
  396.7 170.6 %reduce-scatter.14.cloned.1.call-start = ((), (), s32[]{:S(2)}) async-start(), calls=%async_computation.15 | async-start | bytes 2654208 | tf_op jit(solution)/shard_map/reduce_scatter | solution.py:319
  424.7 51.2 %copy-start.13 = (bf16[768,2304]{1,0:T(8,128)(2,1)S(1)}, bf16[768,2304]{1,0:T(8,128)(2,1)}, u32[]{:S(2)}) copy-start(bf16[768,2304]{1,0:T(8,128)(2,1)} %all-gather.12.cloned.1.call-done) | copy-start | bytes 10616836
  424.7 51.2 %copy-start.28 = (f32[768]{0:T(1024)S(1)}, f32[768]{0:T(1024)}, u32[]{:S(2)}) copy-start(f32[768]{0:T(1024)} %copy-done.27) | copy-start | bytes 9220
  424.7 142.6 %reduce-scatter.24.cloned.1.call-start = ((), (), s32[]{:S(2)}) async-start(), calls=%async_computation.20 | async-start | bytes 2654208
  463.0 7.6 collective-permute-start
  464.9 5.7 collective-permute-start.1
  481.2 120.4 %reduce-scatter.16.cloned.1.call-start = ((), (), s32[]{:S(2)}) async-start(), calls=%async_computation.16 | async-start | bytes 7962624 | tf_op jit(solution)/shard_map/reduce_scatter | solution.py:322
  493.5 176.9 %reduce-scatter.12.cloned.1.call-start = ((), (), s32[]{:S(2)}) async-start(), calls=%async_computation.14 | async-start | bytes 7962624 | tf_op jit(solution)/shard_map/reduce_scatter | solution.py:318
  498.3 252.5 %reduce-scatter.20.cloned.1.call-start = ((), (), s32[]{:S(2)}) async-start(), calls=%async_computation.18 | async-start | bytes 10616832 | tf_op jit(solution)/shard_map/reduce_scatter | solution.py:326
  511.9 319.2 %reduce-scatter.22.cloned.1.call-start = ((), (), s32[]{:S(2)}) async-start(), calls=%async_computation.19 | async-start | bytes 10616832 | tf_op jit(solution)/shard_map/reduce_scatter | solution.py:327
  530.0 30.8 %copy-start.15 = (bf16[768,768]{1,0:T(8,128)(2,1)S(1)}, bf16[768,768]{1,0:T(8,128)(2,1)}, u32[]{:S(2)}) copy-start(bf16[768,768]{1,0:T(8,128)(2,1)} %all-gather.10.cloned.1.call-done) | copy-start | bytes 3538948
  (71 other events, 546.0 us)
Sparse Core Ops, SparseCore 0:
  9.9 26.8 all-gather.9
  38.7 33.9 all-gather.11
  74.6 24.0 all-gather.13
  100.4 33.9 all-gather.15
  136.1 24.0 all-gather.17
  162.0 38.9 all-gather.19
  202.8 38.9 all-gather.21
  396.9 42.4 reduce-scatter.17
  443.1 43.2 reduce-scatter.13
  489.5 42.4 reduce-scatter.23
  536.0 65.4 reduce-scatter.15
  604.9 65.4 reduce-scatter.11
  674.3 76.4 reduce-scatter.19
  754.6 76.4 reduce-scatter.21
where the time goes:
time: 1030 us; the launch traced here: 1020 us
  waiting for transfers between devices  358 us (35%)
  blocking collectives  290 us (28%)
  matrix products  183 us (18%)
  local copies, waits for them, and re-layouts  107 us (10%)
  other arithmetic  55.7 us (5%)
  between operations  19.2 us (2%)
    psum x1, blocking collectives, local(): lax.psum((shares[0], shares[1], shares[2], shares[3], shares[4], shares[5...  178 us
    reduce_scatter x1, waiting for transfers between devices, local(): lax.psum_scatter(weight_grads[11], 'mp', scatter_dimension=0, tiled=True)  80.4 us
    reduce_scatter x1, waiting for transfers between devices, local(): lax.psum_scatter(weight_grads[12], 'mp', scatter_dimension=0, tiled=True)  80.3 us
    reduce_scatter x1, waiting for transfers between devices, local(): lax.psum_scatter(weight_grads[3], 'mp', scatter_dimension=0, tiled=True)  68.9 us
    unnamed x3, blocking collectives  65.8 us
    reduce_scatter x1, waiting for transfers between devices, local(): lax.psum_scatter(weight_grads[7], 'mp', scatter_dimension=0, tiled=True)  33.1 us
    all_gather x1, waiting for transfers between devices, local(): lax.all_gather(fc_out, 'mp', axis=0, tiled=True)  26.3 us
    all_gather x1, waiting for transfers between devices, local(): lax.all_gather(message_qkv, 'mp', axis=0, tiled=True)  24.8 us
  transfers between devices with their start and end apart: 16, of which 9 were waited for; matrix products, arithmetic and copies ran while one was open for 23% of the time, Pallas kernels for 0%

commit v1 on v0

v1 whole, which is shorter than its diff:
```python
import functools

import jax
import jax.numpy as jnp
from jax import lax
from jax.experimental import pallas as pl
from jax.experimental.pallas import tpu as pltpu
from jax.sharding import PartitionSpec as P

HEADS = 12
FPV = 16
EPS = 1e-05
LOGIT_SCALE = 50.0
ROWS = 208
PACK = 128
VMEM = 60 * 1024 * 1024

f32 = jnp.float32
bf16 = jnp.bfloat16
HIGH = lax.Precision.HIGHEST


def nn(a, b, precision=None):
    return jnp.dot(a, b, preferred_element_type=f32, precision=precision)


def nt(a, b, precision=None):
    return lax.dot_general(
        a, b, (((1,), (1,)), ((), ())), preferred_element_type=f32, precision=precision
    )


def norm_parts(x):
    mean = jnp.mean(x, axis=-1, keepdims=True)
    centred = x - mean
    var = jnp.mean(centred * centred, axis=-1, keepdims=True)
    rstd = lax.rsqrt(var + EPS)
    return centred * rstd, rstd


def norm_back(grad, xhat, rstd, gain):
    gy = grad * gain
    return rstd * (
        gy
        - jnp.mean(gy, axis=-1, keepdims=True)
        - xhat * jnp.mean(gy * xhat, axis=-1, keepdims=True)
    )


def sigmoid(x):
    return 0.5 * jnp.tanh(0.5 * x) + 0.5


def lane_masks(dtype):
    lane = lax.broadcasted_iota(jnp.int32, (1, 128), 1)
    low = (lane < 64).astype(f32)
    return low.astype(dtype), (1.0 - low).astype(dtype)


def transpose(x):
    return jnp.transpose(x.astype(f32)).astype(x.dtype)


def pair_probs(q2, k2, valid):
    m0, m1 = lane_masks(bf16)
    qs = q2 * jnp.asarray(0.125, bf16)
    keys = jnp.concatenate([k2 * m0, k2 * m1], axis=0)
    scores = nt(keys, qs)
    count = k2.shape[0]
    out = []
    for j in range(2):
        s = jnp.where(valid, scores[j * count : (j + 1) * count], -1e30)
        e = jnp.exp(s - jnp.max(s, axis=0, keepdims=True))
        out.append(e * (1.0 / jnp.sum(e, axis=0, keepdims=True)))
    return out


def pair_mix(v2, p0, p1):
    vt = transpose(v2)
    mixed = jnp.concatenate([nn(vt[:64], p0), nn(vt[64:], p1)], axis=0)
    return jnp.transpose(mixed)


def pair_back(q2, k2, v2, dm2, p0, p1):
    m0, m1 = lane_masks(bf16)
    count = k2.shape[0]
    lane = lax.broadcasted_iota(jnp.int32, (1, 128), 1) < 64
    eighth = jnp.asarray(0.125, bf16)
    dps = nt(jnp.concatenate([v2 * m0, v2 * m1], axis=0), dm2)
    lows, grads = [], []
    for j, p in enumerate((p0, p1)):
        dp = dps[j * count : (j + 1) * count]
        p_full = p.astype(f32)
        row = jnp.sum(dp * p_full, axis=0, keepdims=True)
        grads.append((p_full * (dp - row)).astype(bf16))
        lows.append(p.astype(bf16))
    dv = nn(jnp.concatenate(lows, axis=0), dm2)
    dk = nn(jnp.concatenate(grads, axis=0), q2 * eighth)
    kt = transpose(k2 * eighth)
    dq = jnp.transpose(
        jnp.concatenate([nn(kt[:64], grads[0]), nn(kt[64:], grads[1])], axis=0)
    )
    return dq, jnp.where(lane, dk[:count], dk[count:]), jnp.where(lane, dv[:count], dv[count:])


def call(body, out_shape, grid, in_specs, out_specs, scratch, flops, bytes_accessed):
    return pl.pallas_call(
        body,
        out_shape=out_shape,
        grid_spec=pltpu.PrefetchScalarGridSpec(
            num_scalar_prefetch=1,
            grid=grid,
            in_specs=in_specs,
            out_specs=out_specs,
            scratch_shapes=scratch,
        ),
        compiler_params=pltpu.CompilerParams(
            dimension_semantics=("arbitrary",) * len(grid), vmem_limit_bytes=VMEM
        ),
        cost_estimate=pl.CostEstimate(
            flops=flops, bytes_accessed=bytes_accessed, transcendentals=0
        ),
    )


ANY = pl.BlockSpec(memory_space=pl.ANY)


def whole(shape):
    return pl.BlockSpec(shape, lambda i, s: (0,) * len(shape))


def per_step(shape):
    return pl.BlockSpec((1,) + shape, lambda i, s: (i,) + (0,) * len(shape))


def sds(shape, dtype):
    return jax.ShapeDtypeStruct(shape, dtype)


class Weights:
    def __init__(self, arrays, places, rows):
        self.arrays = arrays
        self.places = places
        self.rows = rows

    def copies(self, refs, me, sems, first, columns, dst):
        out = []
        for number, (ref, (slot, start, count)) in enumerate(zip(refs, self.places)):
            if slot is None:
                target = dst
            else:
                offset = jnp.bitwise_xor(me, slot) * self.rows + start
                target = dst.at[pl.ds(pl.multiple_of(offset, 16), count), :]
            out.append(
                pltpu.make_async_copy(
                    ref.at[:, pl.ds(first, columns)], target, sems.at[number]
                )
            )
        return out


def run_copies(copies):
    for copy in copies:
        copy.start()
    for copy in copies:
        copy.wait()


def swap(x, axis, size, bit):
    return lax.ppermute(x, axis, [(i, i ^ bit) for i in range(size)])


def gather_weights(x, fast, mp):
    rows = x.shape[0]
    if not fast:
        full = lax.all_gather(x, "mp", axis=0, tiled=True)
        return Weights([full], [(None, 0, rows * mp)], rows)
    half = rows // 2
    own_c = swap(x, "mp", mp, 1)
    from_x = swap(x, "mp", mp, 2)
    from_y = swap(x, "mp", mp, 4)
    diag_a = swap(from_x[:half], "mp", mp, 4)
    diag_b = swap(from_y[half:], "mp", mp, 2)
    arrays = [x, own_c, from_x, from_y, diag_a, diag_b]
    places = [(0, 0, rows), (1, 0, rows), (2, 0, rows), (4, 0, rows), (6, 0, half), (6, half, half)]
    for number in (2, 3, 4, 5):
        slot, start, count = places[number]
        arrays.append(swap(arrays[number], "mp", mp, 1))
        places.append((slot ^ 1, start, count))
    return Weights(arrays, places, rows)


def gather_small(x, fast, videos, mp):
    if not fast:
        return lax.all_gather(x, ("videos", "mp"), axis=0, tiled=True)
    z = lax.axis_index("videos")
    me = lax.axis_index("mp")
    shape = x.shape
    x = x.reshape((1,) * 5 + shape)
    steps = (
        ("videos", videos, 1, z & 1, 1),
        ("videos", videos, 3, (z >> 1) & 1, 0),
        ("mp", mp, 2, (me >> 1) & 1, 3),
        ("mp", mp, 4, (me >> 2) & 1, 2),
        ("mp", mp, 1, me & 1, 4),
    )
    for axis, size, bit, own_bit, place in steps:
        other = swap(x, axis, size, bit)
        first = jnp.where(own_bit == 0, x, other)
        second = jnp.where(own_bit == 0, other, x)
        x = jnp.concatenate([first, second], axis=place)
    return x.reshape((videos * mp * shape[0],) + shape[1:])


def sum_small(x, fast, mp):
    if not fast:
        return lax.psum(x, "mp")
    for bit in (1, 2, 4):
        x = x + swap(x, "mp", mp, bit)
    return x


def gather_videos(x, fast, videos):
    if not fast:
        return lax.all_gather(x, "videos", axis=0, tiled=True)
    z = lax.axis_index("videos")
    for bit, own_bit in ((1, z & 1), (3, (z >> 1) & 1)):
        other = swap(x, "videos", videos, bit)
        x = jnp.concatenate(
            [jnp.where(own_bit == 0, x, other), jnp.where(own_bit == 0, other, x)], axis=0
        )
    return x


def reduce_grad(parts, fast, videos, mp, x_first):
    if not fast:
        share = lax.psum_scatter(parts[0], "mp", scatter_dimension=0, tiled=False)
        return lax.psum(share, "videos").astype(f32)
    keep, send = parts
    other = swap(send, "mp", mp, 1)
    if x_first:
        bits, pick = (2, 4), lambda a, far: a[:, far]
        zbits = (1, 3)
    else:
        bits, pick = (4, 2), lambda a, far: a[far]
        zbits = (3, 1)
    far = (pick(keep, 1).astype(f32) + pick(other, 1).astype(f32)).astype(bf16)
    far = swap(far, "mp", mp, bits[0])
    near = pick(keep, 0).astype(f32) + pick(other, 0).astype(f32) + far.astype(f32)
    far = swap(near[1].astype(bf16), "mp", mp, bits[1])
    total = (near[0] + far.astype(f32)).astype(bf16)
    for bit in zbits:
        other = swap(total, "videos", videos, bit)
        summed = total.astype(f32) + other.astype(f32)
        total = summed.astype(bf16)
    return summed


def message_forward(meta, cls, weights, features):
    rows = cls.shape[0]
    chunk = min(rows, 256)
    count = len(weights.arrays)

    def body(s, cls_ref, *rest):
        pieces, rest = rest[:count], rest[count:]
        act_ref, proj_ref, mix_ref, message_ref, total_ref, params_ref = rest[:6]
        fc_w, qkv_w, out_w, pack_w, sems = rest[6:]

        @pl.when(pl.program_id(0) == 0)
        def _():
            copies = []
            for number, (first, columns, dst) in enumerate(
                (
                    (0, features, fc_w),
                    (features, 3 * features, qkv_w),
                    (4 * features, features, out_w),
                    (5 * features, PACK, pack_w),
                )
            ):
                copies += weights.copies(pieces, s[0], sems.at[number], first, columns, dst)
            run_copies(copies)
            params_ref[...] = jnp.transpose(pack_w[...].astype(f32))[:16]

        ids = cls_ref[:, features:].astype(f32)
        same = ids[:, :1] == jnp.transpose(ids)[:1, :]
        message = nn(cls_ref[:, :features], fc_w[...])
        message_ref[...] = message
        xhat, _ = norm_parts(message)
        act_ref[...] = (xhat * params_ref[0:1] + params_ref[1:2]).astype(bf16)
        proj_ref[...] = nn(act_ref[...], qkv_w[...]).astype(bf16)
        for p in range(HEADS // 2):
            q2, k2, v2 = (
                proj_ref[:, part * features + p * 128 : part * features + (p + 1) * 128]
                for part in range(3)
            )
            p0, p1 = pair_probs(q2, k2, same)
            mix_ref[:, p * 128 : (p + 1) * 128] = pair_mix(
                v2, p0.astype(bf16), p1.astype(bf16)
            ).astype(bf16)
        total_ref[...] = message_ref[...] + nn(mix_ref[...], out_w[...])

    def block(columns):
        return pl.BlockSpec((chunk, columns), lambda i, s: (i, 0))

    return call(
        body,
        [
            sds((rows, features), bf16),
            sds((rows, 3 * features), bf16),
            sds((rows, features), bf16),
            sds((rows, features), f32),
            sds((rows, features), f32),
            sds((16, features), f32),
        ],
        (rows // chunk,),
        [block(features + PACK)] + [ANY] * count,
        [
            block(features),
            block(3 * features),
            block(features),
            block(features),
            block(features),
            whole((16, features)),
        ],
        [
            pltpu.VMEM((features, features), bf16),
            pltpu.VMEM((features, 3 * features), bf16),
            pltpu.VMEM((features, features), bf16),
            pltpu.VMEM((features, PACK), bf16),
            pltpu.SemaphoreType.DMA((4, count)),
        ],
        2 * rows * 5 * features * features,
        12 * features * features,
    )(meta, cls, *weights.arrays)


def attention_forward(meta, frames, total, params, weights):
    number_frames, patches, features = frames.shape
    count = len(weights.arrays)

    def body(s, frames_ref, total_ref, params_ref, *rest):
        pieces, rest = rest[:count], rest[count:]
        act_ref, qkv_ref, probs_ref, mixed_ref, residual_ref = rest[:5]
        qkv_w, out_w, stacked, sems = rest[5:]
        f = pl.program_id(0)

        @pl.when(f == 0)
        def _():
            copies = weights.copies(pieces, s[0], sems.at[0], 0, 3 * features, qkv_w)
            copies += weights.copies(pieces, s[0], sems.at[1], 3 * features, features, out_w)
            run_copies(copies)
            stacked[...] = jnp.zeros_like(stacked)

        stacked[0:patches] = frames_ref[0].astype(f32)
        stacked[patches : patches + 1] = total_ref[pl.ds(f, 1), :]
        xhat, _ = norm_parts(stacked[...])
        act_ref[0] = (xhat * params_ref[2:3] + params_ref[3:4]).astype(bf16)
        qkv_ref[0] = nn(act_ref[0], qkv_w[...]).astype(bf16)
        valid = lax.broadcasted_iota(jnp.int32, (ROWS, 1), 0) < patches + 1
        for p in range(HEADS // 2):
            q2, k2, v2 = (
                qkv_ref[0, :, part * features + p * 128 : part * features + (p + 1) * 128]
                for part in range(3)
            )
            p0, p1 = pair_probs(q2, k2, valid)
            p0, p1 = p0.astype(bf16), p1.astype(bf16)
            probs_ref[0, p, 0] = p0
            probs_ref[0, p, 1] = p1
            mixed_ref[0, :, p * 128 : (p + 1) * 128] = pair_mix(v2, p0, p1).astype(bf16)
        residual_ref[0] = stacked[...] + nn(mixed_ref[0], out_w[...])

    n = number_frames
    return call(
        body,
        [
            sds((n, ROWS, features), bf16),
            sds((n, ROWS, 3 * features), bf16),
            sds((n, HEADS // 2, 2, ROWS, ROWS), bf16),
            sds((n, ROWS, features), bf16),
            sds((n, ROWS, features), f32),
        ],
        (n,),
        [per_step((patches, features)), whole((8, features)), whole((16, features))]
        + [ANY] * count,
        [
            per_step((ROWS, features)),
            per_step((ROWS, 3 * features)),
            per_step((HEADS // 2, 2, ROWS, ROWS)),
            per_step((ROWS, features)),
            per_step((ROWS, features)),
        ],
        [
            pltpu.VMEM((features, 3 * features), bf16),
            pltpu.VMEM((features, features), bf16),
            pltpu.VMEM((ROWS, features), f32),
            pltpu.SemaphoreType.DMA((2, count)),
        ],
        2 * n * ROWS * (4 * features * features + 2 * ROWS * features),
        24 * 1024 * 1024,
    )(meta, frames, total, params, *weights.arrays)


def mlp_forward(meta, residual, params, onehot, win, wout, patches):
    n, _, features = residual.shape
    hidden_units = win.arrays[0].shape[1]
    count_in, count_out = len(win.arrays), len(wout.arrays)
    chunks = hidden_units // features
    videos = onehot.shape[0]

    def body(s, residual_ref, params_ref, onehot_ref, *rest):
        in_pieces, rest = rest[:count_in], rest[count_in:]
        out_pieces, rest = rest[:count_out], rest[count_out:]
        act_ref, pre_ref, hidden_ref, out_ref, sum_ref = rest[:5]
        in_w, out_w, means, in_sems, out_sems = rest[5:]
        f = pl.program_id(0)

        @pl.when(f == 0)
        def _():
            run_copies(
                win.copies(in_pieces, s[0], in_sems, 0, hidden_units, in_w)
                + wout.copies(out_pieces, s[0], out_sems, 0, features, out_w)
            )
            means[...] = jnp.zeros_like(means)

        residual_in = residual_ref[0]
        xhat, _ = norm_parts(residual_in)
        act_ref[0] = (xhat * params_ref[4:5] + params_ref[5:6]).astype(bf16)
        output = residual_in
        for c in range(chunks):
            columns = slice(c * features, (c + 1) * features)
            pre = nn(act_ref[0], in_w[:, columns])
            pre_ref[0, :, columns] = pre.astype(bf16)
            hidden = (pre * sigmoid(1.702 * pre)).astype(bf16)
            hidden_ref[0, :, columns] = hidden
            output = output + nn(hidden, out_w[columns, :])
        out_ref[0] = output[:patches].astype(bf16)
        valid = lax.broadcasted_iota(jnp.int32, (ROWS, 1), 0) < patches
        means[pl.ds(f, 1), :] = jnp.sum(
            jnp.where(valid, output, 0.0), axis=0, keepdims=True
        ) * (1.0 / patches)

        @pl.when(f == n - 1)
        def _():
            sum_ref[...] = nn(onehot_ref[...], means[...], HIGH) * (1.0 / FPV)

    return call(
        body,
        [
            sds((n, ROWS, features), bf16),
            sds((n, ROWS, hidden_units), bf16),
            sds((n, ROWS, hidden_units), bf16),
            sds((n, patches, features), bf16),
            sds((videos, features), f32),
        ],
        (n,),
        [per_step((ROWS, features)), whole((16, features)), whole((videos, 8))]
        + [ANY] * (count_in + count_out),
        [
            per_step((ROWS, features)),
            per_step((ROWS, hidden_units)),
            per_step((ROWS, hidden_units)),
            per_step((patches, features)),
            whole((videos, features)),
        ],
        [
            pltpu.VMEM((features, hidden_units), bf16),
            pltpu.VMEM((hidden_units, features), bf16),
            pltpu.VMEM((8, features), f32),
            pltpu.SemaphoreType.DMA((count_in,)),
            pltpu.SemaphoreType.DMA((count_out,)),
        ],
        4 * n * ROWS * features * hidden_units,
        32 * 1024 * 1024,
    )(meta, residual, params, onehot, *win.arrays, *wout.arrays)


def contrast(meta, pooled, ids_column, ids_row, onehot, group_videos, patches):
    total, features = pooled.shape
    pad = onehot.shape[0]
    videos = total // pad * group_videos
    weight = float(videos * FPV * patches)

    def body(s, pooled_ref, column_ref, row_ref, onehot_ref, loss_ref, grad_ref, back):
        rows = lax.broadcasted_iota(jnp.int32, (total, 1), 0)
        lanes = lax.broadcasted_iota(jnp.int32, (1, total), 1)
        row_valid = lax.rem(rows, pad) < group_videos
        lane_valid = lax.rem(lanes, pad) < group_videos
        row_one = row_valid.astype(f32)
        values = jnp.where(row_valid, pooled_ref[...], 0.0)
        centred = (values - jnp.sum(values, axis=0, keepdims=True) / videos) * row_one
        scale = lax.rsqrt(jnp.sum(centred * centred, axis=1, keepdims=True) + 1e-06)
        embed = centred * scale
        logits = LOGIT_SCALE * nt(embed, embed, HIGH)
        other = jnp.logical_and(rows != lanes, jnp.logical_and(row_valid, lane_valid))
        masked = jnp.where(other, logits, -1e30)
        top = jnp.max(masked, axis=1, keepdims=True)
        e = jnp.where(other, jnp.exp(masked - top), 0.0)
        e_sum = jnp.sum(e, axis=1, keepdims=True)
        e_sum = jnp.where(row_valid, e_sum, 1.0)
        positive = jnp.logical_and(column_ref[:, :1] == row_ref[:1, :], other).astype(f32)
        counts = jnp.sum(positive, axis=1, keepdims=True)
        counts = jnp.where(row_valid, counts, 1.0)
        means = jnp.sum(positive * logits, axis=1, keepdims=True) / counts
        terms = jnp.where(row_valid, top + jnp.log(e_sum) - means, 0.0)
        loss_ref[...] = jnp.broadcast_to(
            jnp.sum(terms, axis=0, keepdims=True) / videos, loss_ref.shape
        )
        logit_grad = (e / e_sum - positive / counts) * (weight / videos)
        embed_grad = LOGIT_SCALE * (
            nn(logit_grad, embed, HIGH)
            + lax.dot_general(
                logit_grad, embed, (((0,), (0,)), ((), ())),
                preferred_element_type=f32, precision=HIGH,
            )
        )
        along = jnp.sum(embed_grad * embed, axis=1, keepdims=True)
        centred_grad = scale * (embed_grad - embed * along) * row_one
        back[...] = (
            centred_grad - jnp.sum(centred_grad, axis=0, keepdims=True) / videos
        ) * row_one
        own = back[pl.ds(pl.multiple_of(s[1] * pad, 8), pad), :]
        grad_ref[...] = lax.dot_general(
            onehot_ref[...], own, (((0,), (0,)), ((), ())),
            preferred_element_type=f32, precision=HIGH,
        ) * (1.0 / (FPV * patches))

    return call(
        body,
        [sds((8, 128), f32), sds((8, features), f32)],
        (1,),
        [whole(pooled.shape), whole(ids_column.shape), whole(ids_row.shape), whole(onehot.shape)],
        [whole((8, 128)), whole((8, features))],
        [pltpu.VMEM(pooled.shape, f32)],
        10**6,
        10**6,
    )(meta, pooled, ids_column, ids_row, onehot)


def mlp_backward(meta, cotangent, frame_grad, pre, residual, params, win, wout):
    n, patches, features = cotangent.shape
    hidden_units = pre.shape[2]
    count_in, count_out = len(win.arrays), len(wout.arrays)
    chunks = hidden_units // features

    def body(s, cot_ref, fg_ref, pre_ref, residual_ref, params_ref, *rest):
        in_pieces, rest = rest[:count_in], rest[count_in:]
        out_pieces, rest = rest[:count_out], rest[count_out:]
        branch_ref, pre_grad_ref, residual_grad_ref, low_ref, norm_ref = rest[:5]
        in_w, out_w, output_grad, in_sems, out_sems = rest[5:]
        f = pl.program_id(0)

        @pl.when(f == 0)
        def _():
            run_copies(
                win.copies(in_pieces, s[0], in_sems, 0, hidden_units, in_w)
                + wout.copies(out_pieces, s[0], out_sems, 0, features, out_w)
            )
            output_grad[...] = jnp.zeros_like(output_grad)
            norm_ref[...] = jnp.zeros_like(norm_ref)

        output_grad[0:patches] = cot_ref[0].astype(f32) + fg_ref[pl.ds(f, 1), :]
        branch_ref[0] = output_grad[...].astype(bf16)
        normed = jnp.zeros((ROWS, features), f32)
        for c in range(chunks):
            columns = slice(c * features, (c + 1) * features)
            hidden_grad = nt(branch_ref[0], out_w[columns, :])
            u = pre_ref[0, :, columns].astype(f32)
            sig = sigmoid(1.702 * u)
            slope = sig * (1.0 + 1.702 * u * (1.0 - sig))
            pre_grad = (hidden_grad * slope).astype(bf16)
            pre_grad_ref[0, :, columns] = pre_grad
            normed = normed + nt(pre_grad, in_w[:, columns])
        xhat, rstd = norm_parts(residual_ref[0])
        norm_ref[0:1] += jnp.sum(normed * xhat, axis=0, keepdims=True)
        norm_ref[1:2] += jnp.sum(normed, axis=0, keepdims=True)
        residual_grad = output_grad[...] + norm_back(normed, xhat, rstd, params_ref[4:5])
        residual_grad_ref[0] = residual_grad
        low_ref[0] = residual_grad.astype(bf16)

    return call(
        body,
        [
            sds((n, ROWS, features), bf16),
            sds((n, ROWS, hidden_units), bf16),
            sds((n, ROWS, features), f32),
            sds((n, ROWS, features), bf16),
            sds((8, features), f32),
        ],
        (n,),
        [
            per_step((patches, features)),
            whole((8, features)),
            per_step((ROWS, hidden_units)),
            per_step((ROWS, features)),
            whole((16, features)),
        ]
        + [ANY] * (count_in + count_out),
        [
            per_step((ROWS, features)),
            per_step((ROWS, hidden_units)),
            per_step((ROWS, features)),
            per_step((ROWS, features)),
            whole((8, features)),
        ],
        [
            pltpu.VMEM((features, hidden_units), bf16),
            pltpu.VMEM((hidden_units, features), bf16),
            pltpu.VMEM((ROWS, features), f32),
            pltpu.SemaphoreType.DMA((count_in,)),
            pltpu.SemaphoreType.DMA((count_out,)),
        ],
        4 * n * ROWS * features * hidden_units,
        36 * 1024 * 1024,
    )(meta, cotangent, frame_grad, pre, residual, params, *win.arrays, *wout.arrays)


def attention_backward(meta, low, qkv, probs, weights, patches):
    n, _, features = low.shape
    count = len(weights.arrays)

    def body(s, low_ref, qkv_ref, probs_ref, *rest):
        pieces, rest = rest[:count], rest[count:]
        grad_ref, out_w, mixed_grad, sems = rest

        @pl.when(pl.program_id(0) == 0)
        def _():
            run_copies(weights.copies(pieces, s[0], sems, 3 * features, features, out_w))

        mixed_grad[...] = nt(low_ref[0], out_w[...]).astype(bf16)
        for p in range(HEADS // 2):
            q2, k2, v2 = (
                qkv_ref[0, :, part * features + p * 128 : part * features + (p + 1) * 128]
                for part in range(3)
            )
            grads = pair_back(
                q2, k2, v2, mixed_grad[:, p * 128 : (p + 1) * 128],
                probs_ref[0, p, 0], probs_ref[0, p, 1],
            )
            for part, grad in enumerate(grads):
                grad_ref[0, :, part * features + p * 128 : part * features + (p + 1) * 128] = (
                    grad.astype(bf16)
                )

    return call(
        body,
        sds((n, ROWS, 3 * features), bf16),
        (n,),
        [
            per_step((ROWS, features)),
            per_step((ROWS, 3 * features)),
            per_step((HEADS // 2, 2, ROWS, ROWS)),
        ]
        + [ANY] * count,
        per_step((ROWS, 3 * features)),
        [
            pltpu.VMEM((features, features), bf16),
            pltpu.VMEM((ROWS, features), bf16),
            pltpu.SemaphoreType.DMA((count,)),
        ],
        2 * n * ROWS * (features * features + 6 * ROWS * features),
        24 * 1024 * 1024,
    )(meta, low, qkv, probs, *weights.arrays)


def stacked_backward(meta, qkv_grad, frames, total, residual_grad, params, weights):
    n, patches, features = frames.shape
    count = len(weights.arrays)

    def body(s, grad_ref, frames_ref, total_ref, residual_grad_ref, params_ref, *rest):
        pieces, rest = rest[:count], rest[count:]
        frames_grad_ref, first_ref, total_grad_ref, norm_ref = rest[:4]
        qkv_w, stacked, sems = rest[4:]
        f = pl.program_id(0)

        @pl.when(f == 0)
        def _():
            run_copies(weights.copies(pieces, s[0], sems, 0, 3 * features, qkv_w))
            stacked[...] = jnp.zeros_like(stacked)
            norm_ref[...] = jnp.zeros_like(norm_ref)
            first_ref[...] = jnp.zeros_like(first_ref)
            total_grad_ref[...] = jnp.zeros_like(total_grad_ref)

        stacked[0:patches] = frames_ref[0].astype(f32)
        stacked[patches : patches + 1] = total_ref[pl.ds(f, 1), :]
        pre_grad = nt(grad_ref[0], qkv_w[...])
        xhat, rstd = norm_parts(stacked[...])
        norm_ref[0:1] += jnp.sum(pre_grad * xhat, axis=0, keepdims=True)
        norm_ref[1:2] += jnp.sum(pre_grad, axis=0, keepdims=True)
        stacked[...] = norm_back(pre_grad, xhat, rstd, params_ref[2:3]) + residual_grad_ref[0]
        frames_grad_ref[0] = stacked[0:patches].astype(bf16)
        first_ref[pl.ds(f, 1), :] = stacked[0:1]
        total_grad_ref[pl.ds(f, 1), :] = stacked[patches : patches + 1]
        stacked[patches : patches + 1] = jnp.zeros((1, features), f32)
        stacked[patches + 1 :] = jnp.zeros((ROWS - patches - 1, features), f32)

    return call(
        body,
        [
            sds((n, patches, features), bf16),
            sds((8, features), f32),
            sds((8, features), f32),
            sds((8, features), f32),
        ],
        (n,),
        [
            per_step((ROWS, 3 * features)),
            per_step((patches, features)),
            whole((8, features)),
            per_step((ROWS, features)),
            whole((16, features)),
        ]
        + [ANY] * count,
        [
            per_step((patches, features)),
            whole((8, features)),
            whole((8, features)),
            whole((8, features)),
        ],
        [
            pltpu.VMEM((features, 3 * features), bf16),
            pltpu.VMEM((ROWS, features), f32),
            pltpu.SemaphoreType.DMA((count,)),
        ],
        2 * n * ROWS * 3 * features * features,
        24 * 1024 * 1024,
    )(meta, qkv_grad, frames, total, residual_grad, params, *weights.arrays)


def message_backward(meta, total_grad, cls, act, proj, mix, message, params, weights, rows, own_chunk):
    total, features = act.shape
    chunk = min(total, 256)
    steps = total // chunk
    count = len(weights.arrays)

    def body(s, tg_ref, cls_ref, act_ref, proj_ref, mix_ref, message_ref, params_ref, *rest):
        pieces, rest = rest[:count], rest[count:]
        fc_ref, qkv_ref, out_ref, norm_ref, class_ref = rest[:5]
        fc_w, qkv_w, out_w, grads, low, fc_sum, qkv_sum, out_sum, sems = rest[5:]
        step = pl.program_id(0)

        @pl.when(step == 0)
        def _():
            copies = []
            for number, (first, columns, dst) in enumerate(
                (
                    (4 * features, features, out_w),
                    (features, 3 * features, qkv_w),
                    (0, features, fc_w),
                )
            ):
                copies += weights.copies(pieces, s[0], sems.at[number], first, columns, dst)
            run_copies(copies)
            norm_ref[...] = jnp.zeros_like(norm_ref)
            fc_sum[...] = jnp.zeros_like(fc_sum)
            qkv_sum[...] = jnp.zeros_like(qkv_sum)
            out_sum[...] = jnp.zeros_like(out_sum)

        pick = (
            lax.broadcasted_iota(jnp.int32, (features, 128), 0)
            == lax.broadcasted_iota(jnp.int32, (features, 128), 1) + s[0] * rows
        ).astype(f32).astype(bf16)

        def own_rows(values):
            return jnp.transpose(nn(values, pick)).astype(bf16)[:rows]

        ids = cls_ref[:, features:].astype(f32)
        same = ids[:, :1] == jnp.transpose(ids)[:1, :]
        tg = tg_ref[...]
        mix_grad = nt(tg, out_w[...]).astype(bf16)
        for p in range(HEADS // 2):
            q2, k2, v2 = (
                proj_ref[:, part * features + p * 128 : part * features + (p + 1) * 128]
                for part in range(3)
            )
            p0, p1 = pair_probs(q2, k2, same)
            parts = pair_back(q2, k2, v2, mix_grad[:, p * 128 : (p + 1) * 128], p0, p1)
            for part, grad in enumerate(parts):
                grads[:, part * features + p * 128 : part * features + (p + 1) * 128] = (
                    grad.astype(bf16)
                )
        out_sum[...] += nn(own_rows(mix_ref[...]), tg)
        qkv_sum[...] += nn(own_rows(act_ref[...]), grads[...])
        normed = nt(grads[...], qkv_w[...])
        xhat, rstd = norm_parts(message_ref[...])
        norm_ref[0:1] += jnp.sum(normed * xhat, axis=0, keepdims=True)
        norm_ref[1:2] += jnp.sum(normed, axis=0, keepdims=True)
        message_grad = tg.astype(f32) + norm_back(normed, xhat, rstd, params_ref[0:1])
        low[...] = message_grad
        fc_sum[...] += nn(own_rows(cls_ref[:, :features]), message_grad.astype(bf16))

        @pl.when(step == s[2])
        def _():
            own = low[pl.ds(pl.multiple_of(s[3], 8), 8), :].astype(bf16)
            class_ref[...] = nt(own, fc_w[...])

        @pl.when(step == steps - 1)
        def _():
            fc_ref[...] = fc_sum[...].astype(bf16)
            qkv_ref[...] = qkv_sum[...].astype(bf16)
            out_ref[...] = out_sum[...].astype(bf16)

    def block(columns):
        return pl.BlockSpec((chunk, columns), lambda i, s: (i, 0))

    return call(
        body,
        [
            sds((rows, features), bf16),
            sds((rows, 3 * features), bf16),
            sds((rows, features), bf16),
            sds((8, features), f32),
            sds((8, features), f32),
        ],
        (steps,),
        [
            block(features),
            block(features + PACK),
            block(features),
            block(3 * features),
            block(features),
            block(features),
            whole((16, features)),
        ]
        + [ANY] * count,
        [
            whole((rows, features)),
            whole((rows, 3 * features)),
            whole((rows, features)),
            whole((8, features)),
            whole((8, features)),
        ],
        [
            pltpu.VMEM((features, features), bf16),
            pltpu.VMEM((features, 3 * features), bf16),
            pltpu.VMEM((features, features), bf16),
            pltpu.VMEM((chunk, 3 * features), bf16),
            pltpu.VMEM((chunk, features), f32),
            pltpu.VMEM((rows, features), f32),
            pltpu.VMEM((rows, 3 * features), f32),
            pltpu.VMEM((rows, features), f32),
            pltpu.SemaphoreType.DMA((3, count)),
        ],
        4 * total * 5 * features * features,
        14 * features * features,
    )(meta, total_grad, cls, act, proj, mix, message, params, *weights.arrays)


def scatter_rows(s, product, rows, fast, mp, refs):
    if not fast:
        for d in range(mp):
            refs[0][d] = product[d * rows : (d + 1) * rows].astype(bf16)
        return
    even = (s[0] & 1) == 0
    for pair in range(mp // 2):
        low = product[2 * pair * rows : (2 * pair + 1) * rows].astype(bf16)
        high = product[(2 * pair + 1) * rows : (2 * pair + 2) * rows].astype(bf16)
        slot = jnp.bitwise_xor(s[0] >> 1, pair)
        refs[0][slot] = jnp.where(even, low, high)
        refs[1][slot] = jnp.where(even, high, low)


def weight_grad(meta, jobs, outs, rows, fast, mp):
    features = jobs[0][0].shape[1]
    tokens = jobs[0][0].shape[0]
    steps = len(jobs)
    copies = 2 if fast else 1
    lefts, rights = [], []
    for left, right, _, _, _ in jobs:
        if all(left is not x for x in lefts):
            lefts.append(left)
        if all(right is not x for x in rights):
            rights.append(right)
    left_of = [next(i for i, x in enumerate(lefts) if x is job[0]) for job in jobs]
    right_of = [next(i for i, x in enumerate(rights) if x is job[1]) for job in jobs]

    def body(s, *refs):
        left_refs, refs = refs[: len(lefts)], refs[len(lefts) :]
        right_refs, refs = refs[: len(rights)], refs[len(rights) :]
        out_refs, scratch = refs[: copies * len(outs)], refs[-1]
        step = pl.program_id(0)
        for number in range(len(lefts)):

            @pl.when(step == left_of.index(number))
            def _(number=number):
                scratch[...] = transpose(left_refs[number][...])

        for number in range(len(rights)):
            for target in range(len(outs)):
                mine = [
                    i for i in range(steps) if right_of[i] == number and jobs[i][3] == target
                ]
                if not mine:
                    continue

                @pl.when(jnp.logical_and(step >= mine[0], step <= mine[-1]))
                def _(number=number, target=target):
                    product = nn(scratch[...], right_refs[number][...])
                    scatter_rows(
                        s, product, rows, fast, mp,
                        out_refs[copies * target : copies * (target + 1)],
                    )

    def index_map(values, make):
        def pick(i, s):
            index = values[0]
            for number in range(1, steps):
                index = jnp.where(i >= number, values[number], index)
            return make(index)

        return pick

    def held(number, of, column):
        values, last = [], None
        for i in range(steps):
            if of[i] == number:
                last = jobs[i][column]
            values.append(last)
        first = next(v for v in values if v is not None)
        return [first if v is None else v for v in values]

    in_specs = [whole((tokens, features)) for _ in lefts]
    for number in range(len(rights)):
        in_specs.append(
            pl.BlockSpec(
                (tokens, features),
                index_map(held(number, right_of, 2), lambda index: (0, index)),
            )
        )
    out_of = [job[3] for job in jobs]
    out_specs, out_shape = [], []
    lead = mp // 2 if fast else mp
    for target, columns in enumerate(outs):
        spec = pl.BlockSpec(
            (lead, rows, features),
            index_map(held(target, out_of, 4), lambda index: (0, 0, index)),
        )
        for _ in range(copies):
            out_specs.append(spec)
            out_shape.append(sds((lead, rows, columns), bf16))
    results = call(
        body,
        out_shape,
        (steps,),
        in_specs,
        out_specs,
        [pltpu.VMEM((features, tokens), bf16)],
        2 * steps * tokens * features * features,
        (2 * steps + 1) * tokens * features * 2,
    )(meta, *lefts, *rights)
    grouped = [results[copies * t : copies * (t + 1)] for t in range(len(outs))]
    if not fast:
        return grouped
    return [[x.reshape((2, 2) + x.shape[1:]) for x in pair] for pair in grouped]


def hidden_weight_grad(meta, branch, hidden, rows, fast, mp):
    tokens, features = branch.shape
    copies = 2 if fast else 1
    width = 2 * rows if fast else features

    def body(s, branch_ref, hidden_ref, *refs):
        scratch = refs[-1]

        @pl.when(pl.program_id(0) == 0)
        def _():
            scratch[...] = transpose(branch_ref[...])

        product = nn(scratch[...], hidden_ref[...]).astype(bf16)
        if fast:
            low, high = product[:, :rows], product[:, rows:]
            even = (s[0] & 1) == 0
            refs[0][0] = jnp.where(even, low, high)
            refs[1][0] = jnp.where(even, high, low)
        else:
            refs[0][...] = product

    if fast:
        right_map = lambda i, s: (0, jnp.bitwise_xor(i, s[0] >> 1))
        out_spec = pl.BlockSpec((1, features, rows), lambda i, s: (i, 0, 0))
        out_shape = sds((mp // 2, features, rows), bf16)
    else:
        right_map = lambda i, s: (0, i)
        out_spec = pl.BlockSpec((features, width), lambda i, s: (0, i))
        out_shape = sds((features, hidden.shape[1]), bf16)
    results = call(
        body,
        [out_shape] * copies,
        (hidden.shape[1] // width,),
        [whole((tokens, features)), pl.BlockSpec((tokens, width), right_map)],
        [out_spec] * copies,
        [pltpu.VMEM((features, tokens), bf16)],
        2 * tokens * features * hidden.shape[1],
        (hidden.shape[1] + features) * tokens * 2,
    )(meta, branch, hidden)
    if not fast:
        return [results[0].reshape(features, mp, rows).transpose(1, 0, 2)]
    return [x.reshape((2, 2) + x.shape[1:]) for x in results]


def local(
    videos,
    mp,
    frames,
    cotangent,
    frame_video,
    group_ids,
    message_fc,
    message_gain,
    message_shift,
    message_qkv,
    message_out,
    pre_gain,
    pre_shift,
    attn_qkv,
    attn_out,
    mlp_gain,
    mlp_shift,
    fc_in,
    fc_out,
):
    n, patches, features = frames.shape
    rows = message_fc.shape[0]
    fast = (videos, mp) == (4, 8)
    z = lax.axis_index("videos")
    me = lax.axis_index("mp")
    group_videos = frame_video.shape[0] // FPV
    pad_videos = -(-group_videos // 8) * 8
    device_rows = 8 * (z * mp + me)
    meta = jnp.stack([me, z, device_rows // 256, lax.rem(device_rows, 256)]).astype(jnp.int32)

    own_video = lax.dynamic_slice_in_dim(frame_video, me * n, n)
    own_video = jnp.concatenate([own_video, jnp.full((8 - n,), -1, own_video.dtype)])
    onehot = (
        (own_video - z * group_videos)[None, :] == jnp.arange(pad_videos)[:, None]
    ).astype(f32)
    cls = jnp.concatenate(
        [
            jnp.pad(frames[:, 0, :], ((0, 8 - n), (0, 0))),
            jnp.broadcast_to(own_video.astype(bf16)[:, None], (8, PACK)),
        ],
        axis=1,
    )
    cls_all = gather_small(cls, fast, videos, mp)
    norms = jnp.stack(
        [message_gain, message_shift, pre_gain, pre_shift, mlp_gain, mlp_shift], axis=1
    )
    message_shard = jnp.concatenate(
        [message_fc, message_qkv, message_out, jnp.pad(norms, ((0, 0), (0, PACK - 6)))], axis=1
    )
    message_w = gather_weights(message_shard, fast, mp)
    attn_w = gather_weights(jnp.concatenate([attn_qkv, attn_out], axis=1), fast, mp)
    in_w = gather_weights(fc_in, fast, mp)
    out_w = gather_weights(fc_out, fast, mp)

    msg_act, msg_proj, msg_mix, message, msg_total, params = message_forward(
        meta, cls_all, message_w, features
    )
    own_total = lax.dynamic_slice_in_dim(msg_total, device_rows, 8)
    pre_act, qkv, probs, mixed, residual = attention_forward(
        meta, frames, own_total, params, attn_w
    )
    mlp_act, hidden_pre, hidden, out_frames, video_part = mlp_forward(
        meta, residual, params, onehot, in_w, out_w, patches
    )
    pooled = gather_videos(sum_small(video_part, fast, mp), fast, videos)
    ids = jnp.pad(group_ids.reshape(videos, group_videos), ((0, 0), (0, pad_videos - group_videos)))
    ids = ids.reshape(-1)
    loss, frame_grad = contrast(
        meta,
        pooled,
        jnp.broadcast_to(ids[:, None], (ids.shape[0], 128)),
        jnp.broadcast_to(ids[None, :], (8, ids.shape[0])),
        onehot,
        group_videos,
        patches,
    )
    branch, pre_grad, residual_grad, low, mlp_norm = mlp_backward(
        meta, cotangent, frame_grad, hidden_pre, residual, params, in_w, out_w
    )
    flat = lambda a: a.reshape(n * ROWS, a.shape[-1])
    out_parts = hidden_weight_grad(meta, flat(branch), flat(hidden), fc_out.shape[0], fast, mp)
    grad_fc_out = reduce_grad(out_parts, fast, videos, mp, True)
    act_flat, pre_flat = flat(mlp_act), flat(pre_grad)
    (in_parts,) = weight_grad(
        meta,
        [(act_flat, pre_flat, c, 0, c) for c in range(fc_in.shape[1] // features)],
        [fc_in.shape[1]],
        rows,
        fast,
        mp,
    )
    grad_fc_in = reduce_grad(in_parts, fast, videos, mp, False)

    qkv_grad = attention_backward(meta, low, qkv, probs, attn_w, patches)
    stacked_flat, qkv_flat, mixed_flat, low_flat = map(flat, (pre_act, qkv_grad, mixed, low))
    first_parts, second_parts = weight_grad(
        meta,
        [
            (stacked_flat, qkv_flat, 0, 0, 0),
            (stacked_flat, qkv_flat, 1, 0, 1),
            (stacked_flat, qkv_flat, 2, 1, 0),
            (mixed_flat, low_flat, 0, 1, 1),
        ],
        [2 * features, 2 * features],
        rows,
        fast,
        mp,
    )
    first_grad = reduce_grad(first_parts, fast, videos, mp, True)
    second_grad = reduce_grad(second_parts, fast, videos, mp, False)

    frames_grad, first_token, total_grad, pre_norm = stacked_backward(
        meta, qkv_grad, frames, own_total, residual_grad, params, attn_w
    )
    payload = jnp.concatenate(
        [total_grad, pre_norm[:2], mlp_norm[:2], jnp.zeros((4, features), f32)], axis=0
    ).astype(bf16)
    payload_all = gather_small(payload, fast, videos, mp).reshape(videos * mp, 16, features)
    total_grads = payload_all[:, :8].reshape(-1, features)
    norm_sums = payload_all[:, 8:12].astype(f32)
    while norm_sums.shape[0] > 1:
        half = norm_sums.shape[0] // 2
        norm_sums = norm_sums[:half] + norm_sums[half:]
    norm_sums = norm_sums[0]
    grad_message_fc, grad_message_qkv, grad_message_out, message_norm, class_grad = (
        message_backward(
            meta, total_grads, cls_all, msg_act, msg_proj, msg_mix, message, params, message_w,
            rows, None,
        )
    )
    tokens = (first_token + class_grad)[:n].astype(bf16)
    frames_grad = lax.dynamic_update_slice(frames_grad, tokens[:, None, :], (0, 0, 0))
    norm_all = jnp.concatenate([message_norm[:2], norm_sums], axis=0)
    norm_own = lax.dynamic_slice_in_dim(norm_all, me * rows, rows, 1).astype(bf16)
    return (
        out_frames,
        loss[0, 0],
        frames_grad,
        grad_message_fc,
        norm_own[0],
        norm_own[1],
        grad_message_qkv,
        grad_message_out,
        norm_own[2],
        norm_own[3],
        jnp.concatenate([first_grad, second_grad[:, :features]], axis=1).astype(bf16),
        second_grad[:, features:].astype(bf16),
        norm_own[4],
        norm_own[5],
        grad_fc_in.astype(bf16),
        grad_fc_out.T.astype(bf16),
    )


def solution(mesh):
    weight, norm = P("mp", None), P("mp")
    frame = P(("videos", "mp"), None, None)
    params = (
        weight, norm, norm, weight, weight, norm, norm, weight, weight, norm, norm, weight, weight,
    )
    return jax.shard_map(
        functools.partial(local, mesh.shape["videos"], mesh.shape["mp"]),
        mesh=mesh,
        in_specs=(frame, frame, P("videos"), P()) + params,
        out_specs=(frame, P(), frame) + params,
        check_vma=False,
    )
```

time: 1030 us -> 494 us (0.48)
  blocking collectives: 290 us -> 0 us
  waiting for transfers between devices: 358 us -> 172 us
  matrix products: 183 us -> 0 us
  Pallas kernels: 0 us -> 180 us
  local copies, waits for them, and re-layouts: 107 us -> 24.9 us
  starting transfers between devices: 5.61 us -> 80.7 us
  other arithmetic: 55.7 us -> 26.4 us
  between operations: 19.2 us -> 2.15 us
    reduce_scatter x6 -> x0, waiting for transfers between devices: 263 us -> none  [the longest x1 80.4 us: local(): lax.psum_scatter(weight_grads[11], 'mp', scatter_dimension=0, tiled=True)]
    psum x2 -> x0, blocking collectives: 202 us -> none  [the longest x1 178 us: local(): lax.psum((shares[0], shares[1], shares[2], shares[3], shares[4], shares[5...]
    dot_general x38 -> x0, matrix products: 183 us -> none  [the longest x1 16.4 us: local(): jnp.einsum('rd,fd->rf', branch_grad, fc_out_b, preferred_element_type=f32)]
    pallas_call x0 -> x11, Pallas kernels: none -> 180 us  [the longest x1 28 us: attention_forward(): call(body, [sds((n, ROWS, features), bf16), sds((n, ROWS, 3 * features),...]
    ppermute x0 -> x71, waiting for transfers between devices: none -> 172 us  [swap(): return lax.ppermute(x, axis, [(i, i ^ bit) for i in range(size)])]
    all_gather x7 -> x0, waiting for transfers between devices: 90.6 us -> none  [the longest x1 26.3 us: local(): lax.all_gather(fc_out, 'mp', axis=0, tiled=True)]
    ppermute x0 -> x71, starting transfers between devices: none -> 80.7 us  [swap(): return lax.ppermute(x, axis, [(i, i ^ bit) for i in range(size)])]
    unnamed x3 -> x0, blocking collectives: 65.8 us -> none
  transfers between devices with their start and end apart: 16 -> 71, of which waited for: 9 -> 34; matrix products, arithmetic and copies ran while one was open for 23% -> 9% of each run, Pallas kernels for 0% -> 18%
where the time goes in v1:
time: 494 us; the launch traced here: 486 us
  Pallas kernels  180 us (36%)
  waiting for transfers between devices  172 us (35%)
  starting transfers between devices  80.7 us (16%)
  other arithmetic  26.4 us (5%)
  local copies, waits for them, and re-layouts  24.9 us (5%)
    ppermute x71, waiting for transfers between devices, swap(): return lax.ppermute(x, axis, [(i, i ^ bit) for i in range(size)])  172 us
    ppermute x71, starting transfers between devices, swap(): return lax.ppermute(x, axis, [(i, i ^ bit) for i in range(size)])  80.7 us
    pallas_call x1, Pallas kernels, attention_forward(): call(body, [sds((n, ROWS, features), bf16), sds((n, ROWS, 3 * features),...  28 us
    pallas_call x1, Pallas kernels, mlp_backward(): call(body, [sds((n, ROWS, features), bf16), sds((n, ROWS, hidden_units),...  27 us
    pallas_call x2, Pallas kernels, weight_grad(): call(body, out_shape, (steps,), in_specs, out_specs, [pltpu.VMEM((feature...  25.4 us
    pallas_call x1, Pallas kernels, mlp_forward(): call(body, [sds((n, ROWS, features), bf16), sds((n, ROWS, hidden_units),...  24.3 us
    pallas_call x1, Pallas kernels, attention_backward(): call(body, sds((n, ROWS, 3 * features), bf16), (n,), [per_step((ROWS, fea...  21.4 us
    pallas_call x1, Pallas kernels, stacked_backward(): call(body, [sds((n, patches, features), bf16), sds((8, features), f32), s...  14.3 us
  transfers between devices with their start and end apart: 71, of which 34 were waited for; matrix products, arithmetic and copies ran while one was open for 9% of the time, Pallas kernels for 18%

profile of v1, /device:TPU:0, one launch (start us, length us, event | category | flops | bytes accessed | tf_op | source)
XLA Modules:
  0.0 486.3 jit_solution(4085368373976888097)
XLA Ops:
  7.2 4.1 collective-permute-start.1
  27.3 8.4 %collective-permute-done.15.rest_2_ = bf16[96,3072]{1,0:T(8,128)(2,1)S(1)} collective-permute-done((bf16[96,3072]{1,0:T(8,128)(2,1)S(1)}, bf16[96,3072]{1,0:T(8,128)(2,1)S(1)}, u32[]{:S(2)}, u32[]{:S(2)}) %collective-permute-start.15) | collective-permute-done | bytes 589856 | tf_op jit(solution)/shard_map/ppermute | solution.py:171
  40.6 7.8 %collective-permute-done.24.rest_2_ = bf16[96,3072]{1,0:T(8,128)(2,1)S(1)} collective-permute-done((bf16[96,3072]{1,0:T(8,128)(2,1)}, bf16[96,3072]{1,0:T(8,128)(2,1)S(1)}, u32[]{:S(2)}, u32[]{:S(2)}) %collective-permute-start.24) | collective-permute-done | bytes 589856 | tf_op jit(solution)/shard_map/ppermute | solution.py:171
  53.1 23.7 %collective-permute-done.33.rest_12_ = bf16[384,768]{1,0:T(8,128)(2,1)S(1)} collective-permute-done((bf16[384,768]{1,0:T(8,128)(2,1)S(1)}, bf16[384,768]{1,0:T(8,128)(2,1)S(1)}, u32[]{:S(2)}, u32[]{:S(2)}) %collective-permute-start.33) | collective-permute-done | bytes 589856 | tf_op jit(solution)/shard_map/ppermute | solution.py:171
  85.3 4.6 collective-permute-done.17.rest_4_
  91.8 4.4 collective-permute-done.26.rest_4_
  97.9 4.6 collective-permute-done.35.rest_14_
  104.3 5.1 %collective-permute-done.8.rest_4_ = bf16[48,3968]{1,0:T(8,128)(2,1)} collective-permute-done((bf16[48,3968]{1,0:T(8,128)(2,1)S(1)}, bf16[48,3968]{1,0:T(8,128)(2,1)}, u32[]{:S(2)}, u32[]{:S(2)}) %collective-permute-start.8) | collective-permute-done | bytes 380960 | tf_op jit(solution)/shard_map/ppermute | solution.py:171
  116.0 10.7 %shard_map.288 = (bf16[256,768]{1,0:T(8,128)(2,1)}, bf16[256,2304]{1,0:T(8,128)(2,1)}, bf16[256,768]{1,0:T(8,128)(2,1)}, f32[256,768]{1,0:T(8,128)}, f32[256,768]{1,0:T(8,128)}, /*index=5*/f32[16,768]{1,0:T(8,128)}) custom-call(s32[4]{0:T(128)} %pad_add_fusion.s, bf16[256,896]{1,0:T(8,128)(2,1)} %bitcast.136, bf16[96,3968]{1,0:T(8,128)(2,1)} %copy-done, ...), custom_call_target="tpu_custom_call" | custom-call | flops 1509949440 | bytes 7077888 | tf_op jit(solution)/shard_map/pallas_call | solution.py:306
  129.7 28.0 %shard_map.289 = (bf16[6,208,768]{2,1,0:T(8,128)(2,1)}, bf16[6,208,2304]{2,1,0:T(8,128)(2,1)}, bf16[6,6,2,208,208]{4,3,2,1,0:T(8,128)(2,1)}, bf16[6,208,768]{2,1,0:T(8,128)(2,1)}, f32[6,208,768]{2,1,0:T(8,128)}) custom-call(s32[4]{0:T(128)} %pad_add_fusion.s, bf16[6,197,768]{2,1,0:T(8,128)(2,1)} %frames_ref.3, ...), custom_call_target="tpu_custom_call" | custom-call | flops 6686244864 | bytes 25165824 | tf_op jit(solution)/shard_map/pallas_call | solution.py:374
  158.9 24.3 %shard_map.290 = (bf16[6,208,768]{2,1,0:T(8,128)(2,1)}, bf16[6,208,3072]{2,1,0:T(8,128)(2,1)}, bf16[6,208,3072]{2,1,0:T(8,128)(2,1)}, bf16[6,197,768]{2,1,0:T(8,128)(2,1)}, f32[8,768]{1,0:T(8,128)}) custom-call(s32[4]{0:T(128)} %pad_add_fusion.s, f32[6,208,768]{2,1,0:T(8,128)} %get-tuple-element.58.residual_ref, f32[16,768]{1,0:T(8,128)} %get-tuple-element.57.params_ref, ...), custom_call_target="tpu_custom_call" | custom-call | flops 11777605632 | bytes 33554432 | tf_op jit(solution)/shard_map/pallas_call | solution.py:447
  193.0 3.8 collective-permute-done.44
  196.9 3.9 collective-permute-start.45
  208.3 27.0 %shard_map.292 = (bf16[6,208,768]{2,1,0:T(8,128)(2,1)}, bf16[6,208,3072]{2,1,0:T(8,128)(2,1)}, f32[6,208,768]{2,1,0:T(8,128)}, bf16[6,208,768]{2,1,0:T(8,128)(2,1)}, f32[8,768]{1,0:T(8,128)}) custom-call(s32[4]{0:T(128)} %pad_add_fusion.s, bf16[6,197,768]{2,1,0:T(8,128)(2,1)} %cot_ref.1, f32[8,768]{1,0:T(8,128)} %get-tuple-element.62.fg_ref, ...), custom_call_target="tpu_custom_call" | custom-call | flops 11777605632 | bytes 37748736 | tf_op jit(solution)/shard_map/pallas_call | solution.py:581
  235.2 21.4 %shard_map.293.grad_ref = bf16[6,208,2304]{2,1,0:T(8,128)(2,1)} custom-call(s32[4]{0:T(128)} %pad_add_fusion.s, bf16[6,208,768]{2,1,0:T(8,128)(2,1)} %get-tuple-element.64.low_ref, bf16[6,208,2304]{2,1,0:T(8,128)(2,1)} %get-tuple-element.65.qkv_ref, bf16[6,6,2,208,208]{4,3,2,1,0:T(8,128)(2,1)} %get-tuple-element.66.probs_ref, bf16[96,3072]{1,0:T(8,128)(2,1)} %copy-done.2, ...), custom_call_target="tpu_custom_call" | custom-call | flops 3864526848 | bytes 25165824 | tf_op jit(solution)/shard_map/pallas_call | solution.py:645
  256.7 14.3 %shard_map.294 = (bf16[6,197,768]{2,1,0:T(8,128)(2,1)}, f32[8,768]{1,0:T(8,128)}, f32[8,768]{1,0:T(8,128)}, f32[8,768]{1,0:T(8,128)}) custom-call(s32[4]{0:T(128)} %pad_add_fusion.s, bf16[6,208,2304]{2,1,0:T(8,128)(2,1)} %shard_map.293.grad_ref, bf16[6,197,768]{2,1,0:T(8,128)(2,1)} %frames_ref.3, f32[8,768]{1,0:T(8,128)} %constant_dynamic-slice_fusion.total_ref, ...), custom_call_target="tpu_custom_call" | custom-call | flops 4416602112 | bytes 25165824 | tf_op jit(solution)/shard_map/pallas_call | solution.py:697
  272.6 4.1 collective-permute-done.46
  276.8 3.6 collective-permute-start.47
  284.3 13.8 %shard_map.296 = (bf16[4,96,1536]{2,1,0:T(8,128)(2,1)}, bf16[4,96,1536]{2,1,0:T(8,128)(2,1)}, bf16[4,96,1536]{2,1,0:T(8,128)(2,1)}, bf16[4,96,1536]{2,1,0:T(8,128)(2,1)}) custom-call(s32[4]{0:T(128)} %pad_add_fusion.s, bf16[1248,768]{1,0:T(8,128)(2,1)} %bitcast.154, bf16[1248,768]{1,0:T(8,128)(2,1)} %bitcast.155, bf16[1248,2304]{1,0:T(8,128)(2,1)} %bitcast.130, ...), custom_call_target="tpu_custom_call" | custom-call | flops 5888802816 | bytes 17252352 | tf_op jit(solution)/shard_map/pallas_call | solution.py:941
  303.8 11.6 %shard_map.297 = (bf16[4,96,3072]{2,1,0:T(8,128)(2,1)}, bf16[4,96,3072]{2,1,0:T(8,128)(2,1)}) custom-call(s32[4]{0:T(128)} %pad_add_fusion.s, bf16[1248,768]{1,0:T(8,128)(2,1)} %bitcast.153, bf16[1248,3072]{1,0:T(8,128)(2,1)} %bitcast.152), custom_call_target="tpu_custom_call" | custom-call | flops 5888802816 | bytes 17252352 | tf_op jit(solution)/shard_map/pallas_call | solution.py:941
  317.5 11.8 %shard_map.298 = (bf16[4,768,384]{2,1,0:T(8,128)(2,1)}, bf16[4,768,384]{2,1,0:T(8,128)(2,1)}) custom-call(s32[4]{0:T(128)} %pad_add_fusion.s, bf16[1248,768]{1,0:T(8,128)(2,1)} %bitcast.156, bf16[1248,3072]{1,0:T(8,128)(2,1)} %bitcast.151), custom_call_target="tpu_custom_call" | custom-call | flops 5888802816 | bytes 9584640 | tf_op jit(solution)/shard_map/pallas_call | solution.py:986
  331.8 4.3 copy.67
  339.0 13.4 %shard_map.295 = (bf16[96,768]{1,0:T(8,128)(2,1)}, bf16[96,2304]{1,0:T(8,128)(2,1)}, bf16[96,768]{1,0:T(8,128)(2,1)}, f32[8,768]{1,0:T(8,128)}, f32[8,768]{1,0:T(8,128)}) custom-call(s32[4]{0:T(128)} %pad_add_fusion.s, bf16[256,768]{1,0:T(8,128)(2,1)} %slice_bitcast_fusion.10.tg_ref, bf16[256,896]{1,0:T(8,128)(2,1)} %bitcast.137, ...), custom_call_target="tpu_custom_call" | custom-call | flops 3019898880 | bytes 8257536 | tf_op jit(solution)/shard_map/pallas_call | solution.py:806
  361.6 10.8 %collective-permute-done.57 = bf16[2,96,1536]{2,1,0:T(8,128)(2,1)} collective-permute-done((bf16[2,96,1536]{2,1,0:T(8,128)(2,1)}, bf16[2,96,1536]{2,1,0:T(8,128)(2,1)}, u32[]{:S(2)}, u32[]{:S(2)}) %collective-permute-start.57) | collective-permute-done | bytes 589856 | tf_op jit(solution)/shard_map/ppermute | solution.py:171
  396.3 3.9 collective-permute-done.54
  402.7 4.3 collective-permute-done.60
  407.1 8.0 %collective-permute-done.62 = bf16[2,96,3072]{2,1,0:T(8,128)(2,1)S(1)} collective-permute-done((bf16[2,96,3072]{2,1,0:T(8,128)(2,1)S(1)}, bf16[2,96,3072]{2,1,0:T(8,128)(2,1)S(1)}, u32[]{:S(2)}, u32[]{:S(2)}) %collective-permute-start.62) | collective-permute-done | bytes 1179680 | tf_op jit(solution)/shard_map/ppermute | solution.py:171
  421.2 9.6 %collective-permute-done.63 = bf16[96,3072]{1,0:T(8,128)(2,1)S(1)} collective-permute-done((bf16[96,3072]{1,0:T(8,128)(2,1)S(1)}, bf16[96,3072]{1,0:T(8,128)(2,1)S(1)}, u32[]{:S(2)}, u32[]{:S(2)}) %collective-permute-start.63) | collective-permute-done | bytes 589856 | tf_op jit(solution)/shard_map/ppermute | solution.py:171
  434.8 14.2 %collective-permute-done.64 = bf16[96,3072]{1,0:T(8,128)(2,1)S(1)} collective-permute-done((bf16[96,3072]{1,0:T(8,128)(2,1)S(1)}, bf16[96,3072]{1,0:T(8,128)(2,1)S(1)}, u32[]{:S(2)}, u32[]{:S(2)}) %collective-permute-start.64) | collective-permute-done | bytes 589856 | tf_op jit(solution)/shard_map/ppermute | solution.py:171
  449.2 9.2 %collective-permute-start.65 = (bf16[96,3072]{1,0:T(8,128)(2,1)S(1)}, bf16[96,3072]{1,0:T(8,128)(2,1)S(1)}, u32[]{:S(2)}, u32[]{:S(2)}) collective-permute-start(bf16[96,3072]{1,0:T(8,128)(2,1)S(1)} %add_convert_fusion.4), channel_id=1, source_target_pairs={{0,8},{8,0},{16,24},{24,16},{1,9},{9,1},{17,25},{25,17},{2,10},{10... | collective-permute-start | bytes 1769480 | tf_op jit(solution)/shard_map/ppermute | solution.py:171
  460.6 11.6 %collective-permute-done.65 = bf16[96,3072]{1,0:T(8,128)(2,1)S(1)} collective-permute-done((bf16[96,3072]{1,0:T(8,128)(2,1)S(1)}, bf16[96,3072]{1,0:T(8,128)(2,1)S(1)}, u32[]{:S(2)}, u32[]{:S(2)}) %collective-permute-start.65) | collective-permute-done | bytes 589856 | tf_op jit(solution)/shard_map/ppermute | solution.py:171
  473.1 11.7 %collective-permute-done.70 = bf16[768,384]{0,1:T(8,128)(2,1)S(1)} collective-permute-done((bf16[768,384]{0,1:T(8,128)(2,1)S(1)}, bf16[768,384]{0,1:T(8,128)(2,1)S(1)}, u32[]{:S(2)}, u32[]{:S(2)}) %collective-permute-start.70) | collective-permute-done | bytes 589856 | tf_op jit(solution)/shard_map/ppermute | solution.py:171
  (315 shorter events, 142.1 us)
Async XLA Ops:
  22.6 16.2 %collective-permute-start.16 = (bf16[96,3072]{1,0:T(8,128)(2,1)S(1)}, bf16[96,3072]{1,0:T(8,128)(2,1)S(1)}, u32[]{:S(2)}, u32[]{:S(2)}) collective-permute-start(bf16[96,3072]{1,0:T(8,128)(2,1)S(1)} %constant_dynamic-update-slice_fusion.rest_0_), channel_id=1, source_target_pairs={{0,4},{1,5},{2,6},{3,7},{4,0},{5,1},{6,2},{7,3},{8,12},{9,13},{10,... | collective-permute-start | bytes 1769480 | tf_op jit(solution)/shard_map/ppermute | solution.py:171
  24.8 23.5 %collective-permute-start.24 = (bf16[96,3072]{1,0:T(8,128)(2,1)}, bf16[96,3072]{1,0:T(8,128)(2,1)S(1)}, u32[]{:S(2)}, u32[]{:S(2)}) collective-permute-start(bf16[96,3072]{1,0:T(8,128)(2,1)} %rest_0_.3), channel_id=1, source_target_pairs={{0,2},{1,3},{2,0},{3,1},{4,6},{5,7},{6,4},{7,5},{8,10},{9,11},{10,... | collective-permute-start | bytes 1769480 | tf_op jit(solution)/shard_map/ppermute | solution.py:171
  26.3 24.6 %collective-permute-start.25 = (bf16[96,3072]{1,0:T(8,128)(2,1)}, bf16[96,3072]{1,0:T(8,128)(2,1)S(1)}, u32[]{:S(2)}, u32[]{:S(2)}) collective-permute-start(bf16[96,3072]{1,0:T(8,128)(2,1)} %rest_0_.3), channel_id=1, source_target_pairs={{0,4},{1,5},{2,6},{3,7},{4,0},{5,1},{6,2},{7,3},{8,12},{9,13},{10,... | collective-permute-start | bytes 1769480 | tf_op jit(solution)/shard_map/ppermute | solution.py:171
  35.7 17.0 %collective-permute-start.32 = (bf16[384,768]{1,0:T(8,128)(2,1)}, bf16[384,768]{1,0:T(8,128)(2,1)S(1)}, u32[]{:S(2)}, u32[]{:S(2)}) collective-permute-start(bf16[384,768]{1,0:T(8,128)(2,1)} %rest_10_.3), channel_id=1, source_target_pairs={{0,1},{1,0},{2,3},{3,2},{4,5},{5,4},{6,7},{7,6},{8,9},{9,8},{10,11... | collective-permute-start | bytes 1769480 | tf_op jit(solution)/shard_map/ppermute | solution.py:171
  38.8 40.2 %collective-permute-start.5 = (bf16[96,3968]{1,0:T(8,128)(2,1)S(1)}, bf16[96,3968]{1,0:T(8,128)(2,1)S(1)}, u32[]{:S(2)}, u32[]{:S(2)}) collective-permute-start(bf16[96,3968]{1,0:T(8,128)(2,1)S(1)} %fusion.10.rest_0_), channel_id=1, source_target_pairs={{0,1},{1,0},{2,3},{3,2},{4,5},{5,4},{6,7},{7,6},{8,9},{9,8},{10,11... | collective-permute-start | bytes 2285576 | tf_op jit(solution)/shard_map/ppermute | solution.py:171
  38.8 41.8 %collective-permute-start.6 = (bf16[96,3968]{1,0:T(8,128)(2,1)S(1)}, bf16[96,3968]{1,0:T(8,128)(2,1)S(1)}, u32[]{:S(2)}, u32[]{:S(2)}) collective-permute-start(bf16[96,3968]{1,0:T(8,128)(2,1)S(1)} %fusion.10.rest_0_), channel_id=1, source_target_pairs={{0,2},{1,3},{2,0},{3,1},{4,6},{5,7},{6,4},{7,5},{8,10},{9,11},{10,... | collective-permute-start | bytes 2285576 | tf_op jit(solution)/shard_map/ppermute | solution.py:171
  48.3 28.5 %collective-permute-start.33 = (bf16[384,768]{1,0:T(8,128)(2,1)S(1)}, bf16[384,768]{1,0:T(8,128)(2,1)S(1)}, u32[]{:S(2)}, u32[]{:S(2)}) collective-permute-start(bf16[384,768]{1,0:T(8,128)(2,1)S(1)} %copy-done.35), channel_id=1, source_target_pairs={{0,2},{1,3},{2,0},{3,1},{4,6},{5,7},{6,4},{7,5},{8,10},{9,11},{10,... | collective-permute-start | bytes 1769480 | tf_op jit(solution)/shard_map/ppermute | solution.py:171
  51.0 26.2 %collective-permute-start.34 = (bf16[384,768]{1,0:T(8,128)(2,1)S(1)}, bf16[384,768]{1,0:T(8,128)(2,1)S(1)}, u32[]{:S(2)}, u32[]{:S(2)}) collective-permute-start(bf16[384,768]{1,0:T(8,128)(2,1)S(1)} %copy-done.35), channel_id=1, source_target_pairs={{0,4},{1,5},{2,6},{3,7},{4,0},{5,1},{6,2},{7,3},{8,12},{9,13},{10,... | collective-permute-start | bytes 1769480 | tf_op jit(solution)/shard_map/ppermute | solution.py:171
  52.7 30.8 %collective-permute-start.7 = (bf16[96,3968]{1,0:T(8,128)(2,1)S(1)}, bf16[96,3968]{1,0:T(8,128)(2,1)S(1)}, u32[]{:S(2)}, u32[]{:S(2)}) collective-permute-start(bf16[96,3968]{1,0:T(8,128)(2,1)S(1)} %fusion.10.rest_0_), channel_id=1, source_target_pairs={{0,4},{1,5},{2,6},{3,7},{4,0},{5,1},{6,2},{7,3},{8,12},{9,13},{10,... | collective-permute-start | bytes 2285576 | tf_op jit(solution)/shard_map/ppermute | solution.py:171
  79.0 17.2 %collective-permute-start.26 = (bf16[48,3072]{1,0:T(8,128)(2,1)S(1)}, bf16[48,3072]{1,0:T(8,128)(2,1)S(1)}, u32[]{:S(2)}, u32[]{:S(2)}) collective-permute-start(bf16[48,3072]{1,0:T(8,128)(2,1)S(1)} %slice.249), channel_id=1, source_target_pairs={{0,4},{1,5},{2,6},{3,7},{4,0},{5,1},{6,2},{7,3},{8,12},{9,13},{10,... | collective-permute-start | bytes 884744 | tf_op jit(solution)/shard_map/ppermute | solution.py:171
  80.6 17.2 %collective-permute-start.27 = (bf16[48,3072]{1,0:T(8,128)(2,1)S(1)}, bf16[48,3072]{1,0:T(8,128)(2,1)S(1)}, u32[]{:S(2)}, u32[]{:S(2)}) collective-permute-start(bf16[48,3072]{1,0:T(8,128)(2,1)S(1)} %slice.250), channel_id=1, source_target_pairs={{0,2},{1,3},{2,0},{3,1},{4,6},{5,7},{6,4},{7,5},{8,10},{9,11},{10,... | collective-permute-start | bytes 884744 | tf_op jit(solution)/shard_map/ppermute | solution.py:171
  83.5 19.0 %collective-permute-start.35 = (bf16[192,768]{1,0:T(8,128)(2,1)S(1)}, bf16[192,768]{1,0:T(8,128)(2,1)S(1)}, u32[]{:S(2)}, u32[]{:S(2)}) collective-permute-start(bf16[192,768]{1,0:T(8,128)(2,1)S(1)} %slice.251), channel_id=1, source_target_pairs={{0,4},{1,5},{2,6},{3,7},{4,0},{5,1},{6,2},{7,3},{8,12},{9,13},{10,... | collective-permute-start | bytes 884744 | tf_op jit(solution)/shard_map/ppermute | solution.py:171
  89.9 21.3 %collective-permute-start.19 = (bf16[96,3072]{1,0:T(8,128)(2,1)S(1)}, bf16[96,3072]{1,0:T(8,128)(2,1)S(1)}, u32[]{:S(2)}, u32[]{:S(2)}) collective-permute-start(bf16[96,3072]{1,0:T(8,128)(2,1)S(1)} %collective-permute-done.15.rest_2_), channel_id=1, source_target_pairs={{0,1},{1,0},{2,3},{3,2},{4,5},{5,4},{6,7},{7,6},{8,9},{9,8},{10,11... | collective-permute-start | bytes 1769480 | tf_op jit(solution)/shard_map/ppermute | solution.py:171
  89.9 19.5 %collective-permute-start.8 = (bf16[48,3968]{1,0:T(8,128)(2,1)S(1)}, bf16[48,3968]{1,0:T(8,128)(2,1)}, u32[]{:S(2)}, u32[]{:S(2)}) collective-permute-start(bf16[48,3968]{1,0:T(8,128)(2,1)S(1)} %slice.245), channel_id=1, source_target_pairs={{0,4},{1,5},{2,6},{3,7},{4,0},{5,1},{6,2},{7,3},{8,12},{9,13},{10,... | collective-permute-start | bytes 1142792 | tf_op jit(solution)/shard_map/ppermute | solution.py:171
  128.1 29.6 %collective-permute-start.37 = (bf16[384,768]{1,0:T(8,128)(2,1)S(1)}, bf16[384,768]{1,0:T(8,128)(2,1)S(1)}, u32[]{:S(2)}, u32[]{:S(2)}) collective-permute-start(bf16[384,768]{1,0:T(8,128)(2,1)S(1)} %copy-done.23), channel_id=1, source_target_pairs={{0,1},{1,0},{2,3},{3,2},{4,5},{5,4},{6,7},{7,6},{8,9},{9,8},{10,11... | collective-permute-start | bytes 1769480 | tf_op jit(solution)/shard_map/ppermute | solution.py:171
  128.6 29.1 %collective-permute-start.38 = (bf16[384,768]{1,0:T(8,128)(2,1)S(1)}, bf16[384,768]{1,0:T(8,128)(2,1)S(1)}, u32[]{:S(2)}, u32[]{:S(2)}) collective-permute-start(bf16[384,768]{1,0:T(8,128)(2,1)S(1)} %copy-done.25), channel_id=1, source_target_pairs={{0,1},{1,0},{2,3},{3,2},{4,5},{5,4},{6,7},{7,6},{8,9},{9,8},{10,11... | collective-permute-start | bytes 1769480 | tf_op jit(solution)/shard_map/ppermute | solution.py:171
  128.8 28.9 %collective-permute-start.31 = (bf16[48,3072]{1,0:T(8,128)(2,1)}, bf16[48,3072]{1,0:T(8,128)(2,1)S(1)}, u32[]{:S(2)}, u32[]{:S(2)}) collective-permute-start(bf16[48,3072]{1,0:T(8,128)(2,1)} %copy-done.41), channel_id=1, source_target_pairs={{0,1},{1,0},{2,3},{3,2},{4,5},{5,4},{6,7},{7,6},{8,9},{9,8},{10,11... | collective-permute-start | bytes 884744 | tf_op jit(solution)/shard_map/ppermute | solution.py:171
  129.2 28.6 %collective-permute-start.39 = (bf16[192,768]{1,0:T(8,128)(2,1)}, bf16[192,768]{1,0:T(8,128)(2,1)}, u32[]{:S(2)}, u32[]{:S(2)}) collective-permute-start(bf16[192,768]{1,0:T(8,128)(2,1)} %copy-done.42), channel_id=1, source_target_pairs={{0,1},{1,0},{2,3},{3,2},{4,5},{5,4},{6,7},{7,6},{8,9},{9,8},{10,11... | collective-permute-start | bytes 884744 | tf_op jit(solution)/shard_map/ppermute | solution.py:171
  129.3 28.5 %collective-permute-start.40 = (bf16[192,768]{1,0:T(8,128)(2,1)}, bf16[192,768]{1,0:T(8,128)(2,1)}, u32[]{:S(2)}, u32[]{:S(2)}) collective-permute-start(bf16[192,768]{1,0:T(8,128)(2,1)} %copy-done.43), channel_id=1, source_target_pairs={{0,1},{1,0},{2,3},{3,2},{4,5},{5,4},{6,7},{7,6},{8,9},{9,8},{10,11... | collective-permute-start | bytes 884744 | tf_op jit(solution)/shard_map/ppermute | solution.py:171
  282.8 19.4 %collective-permute-start.48 = (bf16[2,2,1,1,1,16,768]{6,5,4,3,2,1,0:T(8,128)(2,1)S(1)}, bf16[2,2,1,1,1,16,768]{6,5,4,3,2,1,0:T(8,128)(2,1)S(1)}, u32[]{:S(2)}, u32[]{:S(2)}) collective-permute-start(bf16[2,2,1,1,1,16,768]{6,5,4,3,2,1,0:T(8,128)(2,1)S(1)} %pad_maximum_fusion.8), channel_id=1, source_target_pairs={{0,2},{1,3},{2,0},{3,1},{4,6},{5,7},{6,4},{7,5},{8,10},{9,11},{10,... | collective-permute-start | bytes 294920 | tf_op jit(solution)/shard_map/ppermute | solution.py:171
  299.3 54.9 %collective-permute-start.56 = (bf16[2,2,96,1536]{3,2,1,0:T(8,128)(2,1)}, bf16[2,2,96,1536]{3,2,1,0:T(8,128)(2,1)}, u32[]{:S(2)}, u32[]{:S(2)}) collective-permute-start(bf16[2,2,96,1536]{3,2,1,0:T(8,128)(2,1)} %bitcast.150), channel_id=1, source_target_pairs={{0,1},{1,0},{2,3},{3,2},{4,5},{5,4},{6,7},{7,6},{8,9},{9,8},{10,11... | collective-permute-start | bytes 3538952 | tf_op jit(solution)/shard_map/ppermute | solution.py:171
  301.7 57.9 %collective-permute-start.51 = (bf16[2,2,96,1536]{3,2,0,1:T(8,128)(2,1)}, bf16[2,2,96,1536]{3,2,0,1:T(8,128)(2,1)}, u32[]{:S(2)}, u32[]{:S(2)}) collective-permute-start(bf16[2,2,96,1536]{3,2,0,1:T(8,128)(2,1)} %copy.64), channel_id=1, source_target_pairs={{0,1},{1,0},{2,3},{3,2},{4,5},{5,4},{6,7},{7,6},{8,9},{9,8},{10,11... | collective-permute-start | bytes 3538952 | tf_op jit(solution)/shard_map/ppermute | solution.py:171
  315.4 71.1 %collective-permute-start.61 = (bf16[2,2,96,3072]{3,2,1,0:T(8,128)(2,1)}, bf16[2,2,96,3072]{3,2,1,0:T(8,128)(2,1)}, u32[]{:S(2)}, u32[]{:S(2)}) collective-permute-start(bf16[2,2,96,3072]{3,2,1,0:T(8,128)(2,1)} %bitcast.149), channel_id=1, source_target_pairs={{0,1},{1,0},{2,3},{3,2},{4,5},{5,4},{6,7},{7,6},{8,9},{9,8},{10,11... | collective-permute-start | bytes 7077896 | tf_op jit(solution)/shard_map/ppermute | solution.py:171
  317.0 19.8 %collective-permute-start.50 = (bf16[2,2,2,2,1,16,768]{6,5,4,3,2,1,0:T(8,128)(2,1)}, bf16[2,2,2,2,1,16,768]{6,5,4,3,2,1,0:T(8,128)(2,1)}, u32[]{:S(2)}, u32[]{:S(2)}) collective-permute-start(bf16[2,2,2,2,1,16,768]{6,5,4,3,2,1,0:T(8,128)(2,1)} %pad_maximum_fusion.3), channel_id=1, source_target_pairs={{0,1},{1,0},{2,3},{3,2},{4,5},{5,4},{6,7},{7,6},{8,9},{9,8},{10,11... | collective-permute-start | bytes 1179656 | tf_op jit(solution)/shard_map/ppermute | solution.py:171
  336.1 53.7 %collective-permute-start.66 = (bf16[2,2,768,384]{2,3,0,1:T(8,128)(2,1)}, bf16[2,2,768,384]{2,3,0,1:T(8,128)(2,1)}, u32[]{:S(2)}, u32[]{:S(2)}) collective-permute-start(bf16[2,2,768,384]{2,3,0,1:T(8,128)(2,1)} %copy.67), channel_id=1, source_target_pairs={{0,1},{1,0},{2,3},{3,2},{4,5},{5,4},{6,7},{7,6},{8,9},{9,8},{10,11... | collective-permute-start | bytes 7077896 | tf_op jit(solution)/shard_map/ppermute | solution.py:171
  388.2 26.8 %collective-permute-start.62 = (bf16[2,96,3072]{2,1,0:T(8,128)(2,1)S(1)}, bf16[2,96,3072]{2,1,0:T(8,128)(2,1)S(1)}, u32[]{:S(2)}, u32[]{:S(2)}) collective-permute-start(bf16[2,96,3072]{2,1,0:T(8,128)(2,1)S(1)} %fusion), channel_id=1, source_target_pairs={{0,4},{1,5},{2,6},{3,7},{4,0},{5,1},{6,2},{7,3},{8,12},{9,13},{10,... | collective-permute-start | bytes 3538952 | tf_op jit(solution)/shard_map/ppermute | solution.py:171
  391.4 27.3 %collective-permute-start.67 = (bf16[2,768,384]{1,2,0:T(8,128)(2,1)S(1)}, bf16[2,768,384]{1,2,0:T(8,128)(2,1)S(1)}, u32[]{:S(2)}, u32[]{:S(2)}) collective-permute-start(bf16[2,768,384]{1,2,0:T(8,128)(2,1)S(1)} %fusion.3), channel_id=1, source_target_pairs={{0,2},{1,3},{2,0},{3,1},{4,6},{5,7},{6,4},{7,5},{8,10},{9,11},{10,... | collective-permute-start | bytes 3538952 | tf_op jit(solution)/shard_map/ppermute | solution.py:171
  400.3 32.6 %collective-permute-start.55 = (bf16[96,1536]{1,0:T(8,128)(2,1)S(1)}, bf16[96,1536]{1,0:T(8,128)(2,1)S(1)}, u32[]{:S(2)}, u32[]{:S(2)}) collective-permute-start(bf16[96,1536]{1,0:T(8,128)(2,1)S(1)} %add_convert_fusion.9), channel_id=1, source_target_pairs={{0,24},{8,16},{16,8},{24,0},{1,25},{9,17},{17,9},{25,1},{2,26},{10... | collective-permute-start | bytes 884744 | tf_op jit(solution)/shard_map/ppermute | solution.py:171
  430.9 18.1 %collective-permute-start.64 = (bf16[96,3072]{1,0:T(8,128)(2,1)S(1)}, bf16[96,3072]{1,0:T(8,128)(2,1)S(1)}, u32[]{:S(2)}, u32[]{:S(2)}) collective-permute-start(bf16[96,3072]{1,0:T(8,128)(2,1)S(1)} %fusion.7), channel_id=1, source_target_pairs={{0,24},{8,16},{16,8},{24,0},{1,25},{9,17},{17,9},{25,1},{2,26},{10... | collective-permute-start | bytes 1769480 | tf_op jit(solution)/shard_map/ppermute | solution.py:171
  433.8 25.4 %collective-permute-start.69 = (bf16[768,384]{0,1:T(8,128)(2,1)S(1)}, bf16[768,384]{0,1:T(8,128)(2,1)S(1)}, u32[]{:S(2)}, u32[]{:S(2)}) collective-permute-start(bf16[768,384]{0,1:T(8,128)(2,1)S(1)} %fusion.5), channel_id=1, source_target_pairs={{0,8},{8,0},{16,24},{24,16},{1,9},{9,1},{17,25},{25,17},{2,10},{10... | collective-permute-start | bytes 1769480 | tf_op jit(solution)/shard_map/ppermute | solution.py:171
  449.2 23.0 %collective-permute-start.65 = (bf16[96,3072]{1,0:T(8,128)(2,1)S(1)}, bf16[96,3072]{1,0:T(8,128)(2,1)S(1)}, u32[]{:S(2)}, u32[]{:S(2)}) collective-permute-start(bf16[96,3072]{1,0:T(8,128)(2,1)S(1)} %add_convert_fusion.4), channel_id=1, source_target_pairs={{0,8},{8,0},{16,24},{24,16},{1,9},{9,1},{17,25},{25,17},{2,10},{10... | collective-permute-start | bytes 1769480 | tf_op jit(solution)/shard_map/ppermute | solution.py:171
  459.3 25.5 %collective-permute-start.70 = (bf16[768,384]{0,1:T(8,128)(2,1)S(1)}, bf16[768,384]{0,1:T(8,128)(2,1)S(1)}, u32[]{:S(2)}, u32[]{:S(2)}) collective-permute-start(bf16[768,384]{0,1:T(8,128)(2,1)S(1)} %add_convert_fusion.2), channel_id=1, source_target_pairs={{0,24},{8,16},{16,8},{24,0},{1,25},{9,17},{17,9},{25,1},{2,26},{10... | collective-permute-start | bytes 1769480 | tf_op jit(solution)/shard_map/ppermute | solution.py:171
  (84 other events, 1294.0 us)
